TPU v7x, 256 devices: a whole 4x4x8 slice. The times are simulated.
256 devices in a mesh: expert: 32 (over x, z), dp: 8 (over y, core).
Axes of the slice: x: 4, y: 4, z: 8, core: 2. Of those that a mesh axis runs over, the one named last changes fastest.
Arguments:
- incoming_elements: bfloat16 [33792, 768], P(('expert', 'dp')), may hold values from -6 to 6
- assigned_specialist: int32 [33792, 1], P(('expert', 'dp')), may hold values from 0 to 31; in each aligned block of 132 rows (0 to 131, 132 to 263, ...) at most 9 rows name the same one
- element_couple_kind: int32 [33792], P(('expert', 'dp')), may hold values from 0 to 3, as said below
- chosen_specialist_chance: float32 [33792], P(('expert', 'dp')), may hold values from 0.2 to 1
- specialist_layernorm_multiplier: float32 [768], replicated, may hold values from 0.5 to 1.5
- final_layernorm_multiplier_vec: float32 [768], replicated, may hold values from 0.5 to 1.5
- specialist_first_matrix: bfloat16 [32, 768, 3072], P('expert'), may hold values from -0.21875 to 0.21875
- specialist_second_matrix: bfloat16 [32, 3072, 768], P('expert'), may hold values from -0.109375 to 0.109375
- sharpness_factor: float32 [1], replicated, may hold values from 16 to 48
- similarity_shift_term: float32 [1], replicated, may hold values from -4 to -1
- objective_adjoint_factor: float32 [1], replicated, may hold values from 12288 to 49152
Outputs:
- token_grads: bfloat16 [33792, 768], P(('expert', 'dp'))
- grad_in: bfloat16 [32, 768, 3072], P('expert', None, 'dp')
- grad_out: bfloat16 [32, 3072, 768], P('expert', 'dp')
Inputs may be any that keep to these rules, and one draw needn't show every extreme that they name: `assigned_specialist`: no expert is named by more than 9 rows of one device (aligned blocks of 132 rows), and in some device's rows one expert is named exactly 9 times. `element_couple_kind`: within the rows of one device (aligned blocks of 132 rows), each value k below 2 marks the image tokens of local pair k and appears exactly 50 times; each value k from 2 on marks the text tokens of local pair k - 2 and appears exactly 16 times; the order within a block is arbitrary.
All inputs are finite; a program needn't handle non-finite values.
Results may differ from a plain program's by a relative error of at most 0.019.
Values may be sent and summed in bfloat16 or wider, within the bound.
No kernel may reach another device: no remote copies, remote signals or barrier semaphores. Data moves between devices by JAX's collectives and lax.ppermute only.
A program may use at most 128 MiB of HBM per device.

v0:
```python
import jax
import jax.numpy as jnp
from jax import lax
from jax.experimental import pallas as pl
from jax.experimental.pallas import tpu as pltpu
from jax.sharding import PartitionSpec as P

D = 768
H = 3072
IMG = 50
TXT = 16
E = 32
DP = 8
NX = 4
NZ = 8
TOK = 132
CAP = 9
PAIRS = 512
ROWS = E * CAP
LANES = 128
CHUNKS = D // LANES
SLAB = 56
META = CAP * CHUNKS
TAIL = 16
PACKED = E * SLAB
HB = 1024
HS = H // DP
GROUP = 4 * E

EPS = 1e-06
ROOT_HALF = 0.7071067811865476
INV_ROOT_TAU = 0.3989422804014327
BF = jnp.bfloat16
F32 = jnp.float32


def params(mib):
    return pltpu.CompilerParams(vmem_limit_bytes=mib * 1024 * 1024)


def cost(flops, moved, trans=0):
    return pl.CostEstimate(flops=int(flops), bytes_accessed=int(moved), transcendentals=int(trans))


def dot(a, b, ca=1, cb=0):
    return lax.dot_general(a, b, (((ca,), (cb,)), ((), ())), preferred_element_type=F32)


def norm(values):
    center = values - jnp.mean(values, axis=1, keepdims=True)
    inverse = lax.rsqrt(jnp.mean(center * center, axis=1, keepdims=True) + EPS)
    return center * inverse, inverse


def norm_back(grad_hat, scaled, inverse):
    return inverse * (
        grad_hat
        - jnp.mean(grad_hat, axis=1, keepdims=True)
        - scaled * jnp.mean(grad_hat * scaled, axis=1, keepdims=True)
    )


def gelu_parts(v):
    e = jnp.exp(-0.5 * v * v)
    t = pl.reciprocal(1.0 + (0.3275911 * ROOT_HALF) * jnp.abs(v))
    tail = t * (0.5 * 1.061405429) + (0.5 * -1.453152027)
    tail = t * tail + (0.5 * 1.421413741)
    tail = t * tail + (0.5 * -0.284496736)
    tail = t * tail + (0.5 * 0.254829592)
    tail = t * tail * e
    cdf = jnp.where(v < 0.0, tail, 1.0 - tail)
    return v * cdf, cdf + v * e * INV_ROOT_TAU


def three(v):
    hi = v.astype(BF).astype(F32)
    mid = (v - hi).astype(BF).astype(F32)
    return hi, mid, v - hi - mid


def iota(shape, dim):
    return lax.broadcasted_iota(jnp.int32, shape, dim)


def pack_rows(scr, rows):
    for j in range(CAP):
        for c in range(CHUNKS):
            scr[pl.ds(c * CAP + j, E, stride=SLAB), :] = rows[
                j * E : (j + 1) * E, c * LANES : (c + 1) * LANES
            ]


def unpack_rows(scr, rows):
    for j in range(CAP):
        for c in range(CHUNKS):
            rows[j * E : (j + 1) * E, c * LANES : (c + 1) * LANES] = scr[
                pl.ds(c * CAP + j, E, stride=SLAB), :
            ]


def meta_chance(meta, j):
    return meta[:, j : j + 1] + meta[:, 16 + j : 17 + j] + meta[:, 32 + j : 33 + j]


def fill_hot(hot, meta):
    s, lane = iota((E, GROUP), 0), iota((E, GROUP), 1)
    first = (s % NZ) * (4 * NX) + s // NZ
    marks = [(lane == first + NX * k).astype(F32) for k in range(4)]
    for j in range(CAP):
        rows = jnp.zeros((E, GROUP), F32)
        for k in range(4):
            at = 48 + 16 * k + j
            rows += marks[k] * meta[:, at : at + 1]
        hot[j * E : (j + 1) * E, :GROUP] = rows.astype(BF)


def two(v):
    hi = v.astype(BF)
    return hi, (v - hi.astype(F32)).astype(BF)


VM = pl.BlockSpec(memory_space=pltpu.VMEM)
IN_HBM = pl.BlockSpec(memory_space=pltpu.HBM)
MARK = jax.ShapeDtypeStruct((8, LANES), F32)


def dispatch_kernel(x, route, kind, chance, gain_in, gain_out, out, slot, gains, scr, rows):
    gains[0:1, :] = gain_in[...].reshape(1, D)
    gains[1:2, :] = gain_out[...].reshape(1, D)
    eye = iota((TOK, TOK), 0) == iota((TOK, TOK), 1)

    def column(row):
        return jnp.sum(jnp.where(eye, row, 0.0), axis=1, keepdims=True)

    onehot = (iota((E, TOK), 0) == route[...]).astype(F32)
    upper = (iota((TOK, TOK), 0) <= iota((TOK, TOK), 1)).astype(BF)
    run = dot(onehot.astype(BF), upper)
    pos = jnp.sum(onehot * run, axis=0, keepdims=True) - 1.0
    target = pos * E + route[...].astype(F32)
    placing = (iota((ROWS, TOK), 0) == target.astype(jnp.int32)).astype(F32).astype(BF)
    rows[...] = dot(placing, x[...])

    slot[...] = column(target)
    lane = iota((TOK, LANES), 1)
    field = lane // 16
    hi, mid, low = three(column(chance[...]))
    same = (column(kind[...].astype(F32)).astype(jnp.int32) == field - 3).astype(F32)
    held = jnp.where(
        field == 0, hi, jnp.where(field == 1, mid, jnp.where(field == 2, low, same))
    )
    held = jnp.where(lane % 16 == column(pos).astype(jnp.int32), held, 0.0).astype(BF)
    scr[pl.ds(META, E, stride=SLAB), :] = dot(onehot.astype(BF), held)
    scr[pl.ds(META + 1, E, stride=SLAB), :] = jnp.zeros((E, LANES), F32)
    pack_rows(scr, rows)
    out[...] = scr[...].astype(BF)


def dispatch(x, route, kind, chance, gain_in, gain_out):
    return pl.pallas_call(
        dispatch_kernel,
        out_shape=(
            jax.ShapeDtypeStruct((PACKED, LANES), BF),
            jax.ShapeDtypeStruct((TOK, 1), F32),
            jax.ShapeDtypeStruct((2, D), F32),
        ),
        scratch_shapes=[pltpu.VMEM((PACKED, LANES), F32), pltpu.VMEM((ROWS, D), F32)],
        compiler_params=params(60),
        cost_estimate=cost(2 * ROWS * TOK * D, 700000),
    )(
        x,
        route.reshape(1, TOK),
        kind.reshape(1, TOK),
        chance.reshape(1, TOK),
        gain_in,
        gain_out,
    )


def forward_kernel(
    arr, gains, w1, w2, part, bundle, slope, hot, scaled_in,
    scr, x, normed, acc, w1v, w2v, sem,
):
    cols = [slice(i * HB, (i + 1) * HB) for i in range(H // HB)]
    fetches = [
        (
            pltpu.make_async_copy(w1.at[:, at], w1v.at[:, at], sem.at[0, i]),
            pltpu.make_async_copy(w2.at[at, :], w2v.at[at, :], sem.at[1, i]),
        )
        for i, at in enumerate(cols)
    ]
    for first, second in fetches:
        first.start()
        second.start()
    scr[...] = arr[...].astype(F32)
    unpack_rows(scr, x)
    scaled, inverse = norm(x[...])
    normed[...] = (scaled * gains[0:1, :]).astype(BF)
    scaled_in[...] = scaled.astype(BF)
    for f, v in enumerate(three(inverse)):
        hot[:, GROUP + 3 + f : GROUP + 4 + f] = v.astype(BF)
    for i, at in enumerate(cols):
        fetches[i][0].wait()
        hidden, grad = gelu_parts(dot(normed[...], w1v[:, at]))
        slope[:, at] = grad.astype(BF)
        fetches[i][1].wait()
        term = dot(hidden.astype(BF), w2v[at, :])
        acc[...] = term if i == 0 else acc[...] + term
    meta = scr[pl.ds(META, E, stride=SLAB), :]
    fill_hot(hot, meta)
    lane = iota((E, LANES), 1)
    routing = jnp.where(lane >= 48, meta, 0.0)
    for j in range(CAP):
        at = slice(j * E, (j + 1) * E)
        chance = meta_chance(meta, j)
        mixed = x[at, :] + chance * acc[at, :].astype(BF).astype(F32)
        scaled, inverse = norm(mixed)
        bundle[at, :] = scaled.astype(BF)
        for f, v in enumerate(three(inverse) + three(chance)):
            lane_at = GROUP + f + (3 if f > 2 else 0)
            hot[at, lane_at : lane_at + 1] = v.astype(BF)
        acc[at, :] = scaled * gains[1:2, :]
        for f, v in enumerate(three(chance * inverse)):
            routing = jnp.where(lane == 16 * f + j, v, routing)
    bundle[ROWS:, 2 * LANES :] = jnp.zeros((TAIL, D - 2 * LANES), BF)
    for c in range(E // TAIL):
        bundle[ROWS:, c * LANES : (c + 1) * LANES] = routing[c * TAIL : (c + 1) * TAIL].astype(BF)
    hi, low = two(acc[...])
    part[...] = (dot(hot[:, :GROUP], hi, 0, 0) + dot(hot[:, :GROUP], low, 0, 0)).astype(BF)


def whole(shape):
    return pl.BlockSpec(shape, lambda *_: (0,) * len(shape))


def forward(arr, gains, w1, w2):
    return pl.pallas_call(
        forward_kernel,
        in_specs=[VM, VM, IN_HBM, IN_HBM],
        out_specs=(VM,) * 5,
        out_shape=(
            jax.ShapeDtypeStruct((GROUP, D), BF),
            jax.ShapeDtypeStruct((ROWS + TAIL, D), BF),
            jax.ShapeDtypeStruct((ROWS, H), BF),
            jax.ShapeDtypeStruct((ROWS, 2 * GROUP), BF),
            jax.ShapeDtypeStruct((ROWS, D), BF),
        ),
        scratch_shapes=[
            pltpu.VMEM((PACKED, LANES), F32),
            pltpu.VMEM((ROWS, D), F32),
            pltpu.VMEM((ROWS, D), BF),
            pltpu.VMEM((ROWS, D), F32),
            pltpu.VMEM((D, H), BF),
            pltpu.VMEM((H, D), BF),
            pltpu.SemaphoreType.DMA((2, H // HB)),
        ],
        compiler_params=params(48),
        cost_estimate=cost(4 * ROWS * D * H, 4 * D * H, 2 * ROWS * H),
    )(arr, gains, w1, w2)


HALF = PAIRS // DP


def load_units(near, far, unit, inverse, img, txt, keep):
    for i in range(DP):
        src = near if i < DP // 2 else far
        first = (i % (DP // 2)) * GROUP
        pooled = src[first : first + GROUP, :].astype(F32)
        inv = lax.rsqrt(jnp.sum(pooled * pooled, axis=1, keepdims=True) + EPS)
        u = pooled * inv
        if i < keep:
            unit[i * GROUP : (i + 1) * GROUP, :] = u
            inverse[i * GROUP : (i + 1) * GROUP, :] = inv
        u = u.reshape(NZ, 2 * NZ, D)
        img[i * HALF : (i + 1) * HALF, :] = u[:, :NZ].reshape(HALF, D).astype(BF)
        txt[i * HALF : (i + 1) * HALF, :] = u[:, NZ:].reshape(HALF, D).astype(BF)


def slopes(scalars, products):
    sharpness, shift, factor = scalars[0], scalars[1], scalars[2]
    logits = sharpness * products + shift
    diagonal = iota(products.shape, 0) == iota(products.shape, 1)
    sign = jnp.where(diagonal, 1.0, -1.0)
    return (-(factor / PAIRS) * sharpness) * sign * jax.nn.sigmoid(-sign * logits)


def pool_grads(g_img, g_txt, u, inv, gain):
    a, b = g_img.reshape(NZ, NZ, D), g_txt.reshape(NZ, NZ, D)
    grad = jnp.concatenate([a, b], axis=1).reshape(GROUP, D)
    share = jnp.where(iota((NZ, 2 * NZ, 1), 1) < NZ, 1.0 / IMG, 1.0 / TXT).reshape(GROUP, 1)
    return (inv * share) * (grad - u * jnp.sum(u * grad, axis=1, keepdims=True)) * gain


def own_loss_kernel(scalars, near, far, gains, own, unit, inverse, img, txt):
    load_units(near, far, unit, inverse, img, txt, 1)

    def side(mine, others):
        hi, low = two(slopes(scalars, dot(mine[:HALF, :], others[...], 1, 1)))
        both = dot(jnp.concatenate([hi, low], axis=0), others[...])
        return both[:HALF] + both[HALF:]

    own[...] = pool_grads(side(img, txt), side(txt, img), unit[...], inverse[...], gains[1:2, :])


def all_loss(scalars, near, far, gains, every, unit, inverse, img, txt):
    load_units(near, far, unit, inverse, img, txt, DP)
    slope = slopes(scalars, dot(img[...], txt[...], 1, 1)).astype(BF)
    g_img = dot(slope, txt[...])
    g_txt = dot(slope, img[...], 0, 0)
    for i in range(DP):
        at, half = slice(i * GROUP, (i + 1) * GROUP), slice(i * HALF, (i + 1) * HALF)
        every[i] = pool_grads(
            g_img[half], g_txt[half], unit[at, :], inverse[at, :], gains[1:2, :]
        ).astype(BF)


def merge_kernel(a, b, c, d, out):
    for i, piece in enumerate((a, b, c, d)):
        out[i * GROUP : (i + 1) * GROUP, :] = piece[...]


def merge(pieces):
    return pl.pallas_call(
        merge_kernel,
        out_shape=jax.ShapeDtypeStruct((DP // 2 * GROUP, D), BF),
        compiler_params=params(8),
    )(*pieces)


def own_loss(scalars, near, far, gains):
    return pl.pallas_call(
        own_loss_kernel,
        in_specs=[pl.BlockSpec(memory_space=pltpu.SMEM)] + [VM] * 3,
        out_specs=VM,
        out_shape=jax.ShapeDtypeStruct((GROUP, D), F32),
        scratch_shapes=[
            pltpu.VMEM((GROUP, D), F32),
            pltpu.VMEM((GROUP, 1), F32),
            pltpu.VMEM((PAIRS, D), BF),
            pltpu.VMEM((PAIRS, D), BF),
        ],
        compiler_params=params(24),
        cost_estimate=cost(6 * GROUP * PAIRS * D, 3000000, GROUP * PAIRS),
    )(scalars, near, far, gains)


def backward_kernel(
    bundle, hot, scaled_in, grads, gains, slope, w1, w2, out, mark,
    scr, mixed, rows, acc,
):
    hi, low = two(grads[...])
    mixed[...] = dot(hot[:, :GROUP], hi) + dot(hot[:, :GROUP], low)

    def column(at, n):
        return jnp.sum(hot[at, GROUP + 3 * n : GROUP + 3 * n + 3].astype(F32), axis=1, keepdims=True)

    for j in range(CAP):
        at = slice(j * E, (j + 1) * E)
        grad = norm_back(mixed[at, :], bundle[at, :].astype(F32), column(at, 0))
        mixed[at, :] = grad
        rows[at, :] = (column(at, 2) * grad).astype(BF)
    for i in range(H // HB):
        at = slice(i * HB, (i + 1) * HB)
        hidden = (dot(rows[...], w2[at, :], 1, 1) * slope[:, at].astype(F32)).astype(BF)
        term = dot(hidden, w1[:, at], 1, 1)
        acc[...] = term if i == 0 else acc[...] + term
    for j in range(CAP):
        at = slice(j * E, (j + 1) * E)
        back = acc[at, :].astype(BF).astype(F32) * gains[0:1, :]
        mixed[at, :] += norm_back(back, scaled_in[at, :].astype(F32), column(at, 1))
    for row in (META, META + 1):
        scr[pl.ds(row, E, stride=SLAB), :] = jnp.zeros((E, LANES), F32)
    pack_rows(scr, mixed)
    out[...] = scr[...].astype(BF)
    mark[...] = jnp.zeros_like(mark)


def backward(bundle, hot, scaled_in, grads, gains, slope, w1, w2):
    return pl.pallas_call(
        backward_kernel,
        in_specs=[VM] * 8,
        out_specs=(VM, VM),
        out_shape=(jax.ShapeDtypeStruct((PACKED, LANES), BF), MARK),
        scratch_shapes=[
            pltpu.VMEM((PACKED, LANES), F32),
            pltpu.VMEM((ROWS, D), F32),
            pltpu.VMEM((ROWS, D), BF),
            pltpu.VMEM((ROWS, D), F32),
        ],
        compiler_params=params(24),
        cost_estimate=cost(4 * ROWS * D * H, 4 * D * H + 2 * ROWS * H),
    )(bundle, hot, scaled_in, grads, gains, slope, w1, w2)


def slice_kernel(
    dp, arr, gains, w1, pooled, normed_t, hidden_t, slope, passed, scr, x, normed, hidden, w1s, sem
):
    step = pl.program_id(0)
    at = pl.ds(pl.multiple_of(dp[0] * HS, HS), HS)
    copy = pltpu.make_async_copy(w1.at[:, at], w1s, sem)

    @pl.when(step == 0)
    def _():
        copy.start()
        passed[...] = pooled[...]

    scr[...] = arr[0].astype(F32)
    unpack_rows(scr, x)
    scaled, _inverse = norm(x[...])
    rows = (scaled * gains[0:1, :]).astype(BF)
    at = pl.ds(pl.multiple_of(step * ROWS, ROWS), ROWS)
    normed[at, :] = rows

    @pl.when(step == 0)
    def _():
        copy.wait()

    value, grad = gelu_parts(dot(rows, w1s[...]))
    hidden[at, :] = value.astype(BF)
    slope[...] = grad.astype(BF)

    @pl.when(step == pl.num_programs(0) - 1)
    def _():
        normed_t[...] = normed[...].T
        hidden_t[...] = hidden[...].T


ALL = DP * ROWS


def hidden_slice(dp, arrs, gains, w1, pooled):
    return pl.pallas_call(
        slice_kernel,
        grid_spec=pltpu.PrefetchScalarGridSpec(
            num_scalar_prefetch=1,
            grid=(DP,),
            in_specs=[
                pl.BlockSpec((1, PACKED, LANES), lambda h, dp: (h, 0, 0)),
                whole((2, D)),
                IN_HBM,
                whole((GROUP, D)),
            ],
            out_specs=(
                whole((D, ALL)),
                whole((HS, ALL)),
                pl.BlockSpec((ROWS, HS), lambda h, dp: (h, 0)),
                whole((GROUP, D)),
            ),
            scratch_shapes=[
                pltpu.VMEM((PACKED, LANES), F32),
                pltpu.VMEM((ROWS, D), F32),
                pltpu.VMEM((ALL, D), BF),
                pltpu.VMEM((ALL, HS), BF),
                pltpu.VMEM((D, HS), BF),
                pltpu.SemaphoreType.DMA,
            ],
        ),
        out_shape=(
            jax.ShapeDtypeStruct((D, ALL), BF),
            jax.ShapeDtypeStruct((HS, ALL), BF),
            jax.ShapeDtypeStruct((ALL, HS), BF),
            jax.ShapeDtypeStruct((GROUP, D), BF),
        ),
        compiler_params=params(40),
        cost_estimate=cost(2 * ALL * D * HS, 12000000, 2 * ALL * HS),
    )(dp, arrs, gains, w1, pooled)


def weights_kernel(
    dp, scalars, near, far, gains, bundle, slope, _, normed_t, hidden_t, w2, g_in, g_out, mark,
    hot, rows, hidden, normed, value, w2s, every, unit, inverse, img, txt, sem,
):
    step = pl.program_id(0)
    at = pl.ds(pl.multiple_of(dp[0] * HS, HS), HS)
    weights = pltpu.make_async_copy(w2.at[at, :], w2s, sem.at[0])
    late = [
        pltpu.make_async_copy(normed_t, normed, sem.at[1]),
        pltpu.make_async_copy(hidden_t, value, sem.at[2]),
    ]

    @pl.when(step == 0)
    def _():
        weights.start()
        for copy in late:
            copy.start()
        all_loss(scalars, near, far, gains, every, unit, inverse, img, txt)
        weights.wait()

    for b in range(2):
        meta = bundle[b, ROWS:, : 2 * LANES].astype(F32)
        meta = jnp.concatenate([meta[:, :LANES], meta[:, LANES:]], axis=0)
        fill_hot(hot, meta)
        place = (step ^ lax.div(dp[0], 2)) + 4 * (b ^ lax.rem(dp[0], 2))
        q = dot(hot[...], every[place])
        for j in range(CAP):
            at = slice(j * E, (j + 1) * E)
            grad = norm_back(q[at, :], bundle[b, at, :].astype(F32), meta_chance(meta, j))
            first = pl.multiple_of((2 * step + b) * ROWS + j * E, E)
            rows[pl.ds(first, E), :] = grad.astype(BF)
    at = pl.ds(pl.multiple_of(step * (2 * ROWS), 2 * ROWS), 2 * ROWS)
    hidden[at, :] = (dot(rows[at, :], w2s[...], 1, 1) * slope[...].astype(F32)).astype(BF)

    @pl.when(step == pl.num_programs(0) - 1)
    def _():
        for copy in late:
            copy.wait()
        g_in[...] = dot(normed[...], hidden[...]).astype(BF)
        g_out[...] = dot(value[...], rows[...]).astype(BF)
        mark[...] = jnp.zeros_like(mark)


def weight_grads(dp, scalars, near, far, gains, bundles, slope, after, normed_t, hidden_t, w2):
    return pl.pallas_call(
        weights_kernel,
        grid_spec=pltpu.PrefetchScalarGridSpec(
            num_scalar_prefetch=2,
            grid=(DP // 2,),
            in_specs=[
                whole((DP // 2 * GROUP, D)),
                whole((DP // 2 * GROUP, D)),
                whole((2, D)),
                pl.BlockSpec((2, ROWS + TAIL, D), lambda h, *_: (h, 0, 0)),
                pl.BlockSpec((2 * ROWS, HS), lambda h, *_: (h, 0)),
                whole(MARK.shape),
                IN_HBM,
                IN_HBM,
                IN_HBM,
            ],
            out_specs=(whole((D, HS)), whole((HS, D)), whole(MARK.shape)),
            scratch_shapes=[
                pltpu.VMEM((ROWS, GROUP), BF),
                pltpu.VMEM((ALL, D), BF),
                pltpu.VMEM((ALL, HS), BF),
                pltpu.VMEM((D, ALL), BF),
                pltpu.VMEM((HS, ALL), BF),
                pltpu.VMEM((HS, D), BF),
                pltpu.VMEM((DP, GROUP, D), BF),
                pltpu.VMEM((DP * GROUP, D), F32),
                pltpu.VMEM((DP * GROUP, 1), F32),
                pltpu.VMEM((PAIRS, D), BF),
                pltpu.VMEM((PAIRS, D), BF),
                pltpu.SemaphoreType.DMA((3,)),
            ],
        ),
        out_shape=(
            jax.ShapeDtypeStruct((D, HS), BF),
            jax.ShapeDtypeStruct((HS, D), BF),
            MARK,
        ),
        compiler_params=params(57),
        cost_estimate=cost(6 * ALL * D * HS + 10 * PAIRS * PAIRS * D, 15000000),
    )(dp, scalars, near, far, gains, bundles, slope, after, normed_t, hidden_t, w2)


def collect_kernel(arr, slot, _, out, scr, rows):
    scr[...] = arr[...].astype(F32)
    unpack_rows(scr, rows)
    taking = (iota((TOK, ROWS), 1) == slot[...].astype(jnp.int32)).astype(F32).astype(BF)
    out[...] = dot(taking, rows[...].astype(BF)).astype(BF)


def collect(arr, slot, after):
    return pl.pallas_call(
        collect_kernel,
        out_shape=jax.ShapeDtypeStruct((TOK, D), BF),
        scratch_shapes=[pltpu.VMEM((PACKED, LANES), F32), pltpu.VMEM((ROWS, D), F32)],
        compiler_params=params(16),
        cost_estimate=cost(2 * ROWS * TOK * D, 700000),
    )(arr, slot, after)


Z_GROUPS = [[x * NZ + z for z in range(NZ)] for x in range(NX)]


def to_experts(packed):
    slabs = packed.reshape(E, SLAB, LANES)
    slabs = lax.all_to_all(slabs, "expert", split_axis=0, concat_axis=0, tiled=True)
    return slabs.reshape(PACKED, LANES)


def along_z(values):
    return lax.all_to_all(
        values, "expert", split_axis=0, concat_axis=0, tiled=True, axis_index_groups=Z_GROUPS
    )


def swap(values, axis, size, by):
    return lax.ppermute(values, axis, [(i, i ^ by) for i in range(size)])


def on_device(
    incoming_elements,
    assigned_specialist,
    element_couple_kind,
    chosen_specialist_chance,
    specialist_layernorm_multiplier,
    final_layernorm_multiplier_vec,
    specialist_first_matrix,
    specialist_second_matrix,
    sharpness_factor,
    similarity_shift_term,
    objective_adjoint_factor,
):
    w1 = specialist_first_matrix[0]
    w2 = specialist_second_matrix[0]
    dp = lax.axis_index("dp").astype(jnp.int32).reshape(1)

    packed, slot, gains = dispatch(
        incoming_elements,
        assigned_specialist,
        element_couple_kind,
        chosen_specialist_chance,
        specialist_layernorm_multiplier,
        final_layernorm_multiplier_vec,
    )
    arr = to_experts(packed)
    arrs = lax.all_gather(arr, "dp", axis=0)
    part, bundle, slope, hot, scaled_in = forward(arr, gains, w1, w2)
    bundles = lax.all_gather(bundle, "dp", axis=0)

    part = along_z(part.reshape(NZ, 2 * NZ, D))
    part = jnp.sum(part.astype(F32), axis=0)
    others = [swap(part, "expert", E, NZ * m) for m in range(1, NX)]
    share = jnp.where(jnp.arange(2 * NZ) < NZ, 1.0 / IMG, 1.0 / TXT).astype(F32)
    pooled = (((part + others[0]) + (others[1] + others[2])) * share[:, None]).astype(BF)
    pooled = along_z(jnp.broadcast_to(pooled[None], (NZ, 2 * NZ, D))).reshape(GROUP, D)
    normed_t, hidden_t, grads, passed = hidden_slice(dp, arrs, gains, w1, pooled)
    near = merge([passed] + [swap(pooled, "dp", DP, m) for m in (2, 4, 6)])
    far = swap(near, "dp", DP, 1)

    scalars = jnp.concatenate([sharpness_factor, similarity_shift_term, objective_adjoint_factor])
    own = own_loss(scalars, near, far, gains)
    packed, mark = backward(bundle, hot, scaled_in, own, gains, slope, w1, w2)
    returned = to_experts(packed)
    grad_in, grad_out, mark = weight_grads(
        dp, scalars, near, far, gains, bundles, grads, mark, normed_t, hidden_t, w2
    )
    token_grads = collect(returned, slot, mark)
    return (token_grads, grad_in[None], grad_out[None])


def solution(mesh):
    return jax.shard_map(
        on_device,
        mesh=mesh,
        in_specs=(
            P(("expert", "dp"), None),
            P(("expert", "dp"), None),
            P(("expert", "dp")),
            P(("expert", "dp")),
            P(),
            P(),
            P("expert", None, None),
            P("expert", None, None),
            P(),
            P(),
            P(),
        ),
        out_specs=(P(("expert", "dp"), None), P("expert", None, "dp"), P("expert", "dp", None)),
        check_vma=False,
    )
```

profile of v0, /device:TPU:1, one launch (start us, length us, event | category | flops | bytes accessed | tf_op | source)
XLA Modules:
  0.0 142.5 jit_solution(13690786540918470449)
XLA Ops:
  7.2 0.0 all-gather.4.cloned.1.call-start
  7.2 2.2 %shard_map.130 = (bf16[1792,128]{1,0:T(8,128)(2,1)}, f32[132,1]{1,0:T(8,128)}, f32[2,768]{1,0:T(2,128)}) custom-call(bf16[132,768]{1,0:T(8,128)(2,1)} %x.1, s32[1,132]{1,0:T(1,128)} %bitcast.33, s32[1,132]{1,0:T(1,128)} %bitcast.34, f32[1,132]{1,0:T(1,128)} %bitcast.35, f32[768]{0:T(1024)} %gain_in.1, f32[768]{0:T(1024)} %gain_out.1), custom_call_target="tpu_custom_call" | custom-call | flops 58392576 | bytes 700000 | tf_op jit(solution)/shard_map/pallas_call | solution.py:159
  9.4 24.9 %all_to_all.20 = bf16[32,56,128]{2,1,0:T(8,128)(2,1)} all-to-all(bf16[32,56,128]{2,1,0:T(8,128)(2,1)} %bitcast.32), channel_id=1, replica_groups=mesh['expert'=32,'dp'=8] {'expert'}, dimensions={0} | all-to-all | bytes 917504 | tf_op jit(solution)/shard_map/all_to_all | solution.py:577
  34.3 0.0 all-gather.4.cloned.1.call-update
  34.3 0.0 all-gather.6.cloned.1.call-start
  34.4 1.0 copy-done.3
  35.4 0.7 copy-done.6
  36.1 9.2 %shard_map.131 = (bf16[128,768]{1,0:T(8,128)(2,1)S(1)}, bf16[304,768]{1,0:T(8,128)(2,1)}, bf16[288,3072]{1,0:T(8,128)(2,1)S(1)}, bf16[288,256]{1,0:T(8,128)(2,1)S(1)}, bf16[288,768]{1,0:T(8,128)(2,1)S(1)}) custom-call(bf16[1792,128]{1,0:T(8,128)(2,1)S(1)} %bitcast.25, f32[2,768]{1,0:T(2,128)S(1)} %copy-done.6, bf16[768,3072]{1,0:T(8,128)(2,1)} %bitcast.16, ...), custom_call_target="tpu_custom_call" | custom-call | flops 2717908992 | bytes 9437184 | tf_op jit(solution)/shard_map/pallas_call | solution.py:236
  45.3 0.0 all-gather.6.cloned.1.call-update
  45.3 14.2 %all_to_all.21 = bf16[8,16,768]{2,1,0:T(8,128)(2,1)S(1)} all-to-all(bf16[8,16,768]{2,1,0:T(8,128)(2,1)S(1)} %bitcast.31), channel_id=1, replica_groups={{0,8,16,24,32,40,48,56},{64,72,80,88,96,104,112,120},{128,136,144,152,1..., dimensions={0} | all-to-all | bytes 393216 | tf_op jit(solution)/shard_map/all_to_all | solution.py:582
  59.6 1.7 %collective-permute-start.1 = (f32[16,768]{1,0:T(8,128)S(1)}, f32[16,768]{1,0:T(8,128)S(1)}, u32[]{:S(2)}, u32[]{:S(2)}) collective-permute-start(f32[16,768]{1,0:T(8,128)S(1)} %convert_reduce_fusion), channel_id=1, source_target_pairs={{0,128},{8,136},{16,144},{24,152},{32,160},{40,168},{48,176},{56,1... | collective-permute-start | bytes 147464 | tf_op jit(solution)/shard_map/ppermute | solution.py:588
  61.3 1.5 %collective-permute-start.2 = (f32[16,768]{1,0:T(8,128)S(1)}, f32[16,768]{1,0:T(8,128)S(1)}, u32[]{:S(2)}, u32[]{:S(2)}) collective-permute-start(f32[16,768]{1,0:T(8,128)S(1)} %convert_reduce_fusion), channel_id=1, source_target_pairs={{0,192},{8,200},{16,208},{24,216},{32,224},{40,232},{48,240},{56,2... | collective-permute-start | bytes 147464 | tf_op jit(solution)/shard_map/ppermute | solution.py:588
  62.8 0.0 collective-permute-start
  62.8 1.4 collective-permute-done.1
  64.2 1.7 %collective-permute-done.2 = f32[16,768]{1,0:T(8,128)S(1)} collective-permute-done((f32[16,768]{1,0:T(8,128)S(1)}, f32[16,768]{1,0:T(8,128)S(1)}, u32[]{:S(2)}, u32[]{:S(2)}) %collective-permute-start.2) | collective-permute-done | bytes 49184 | tf_op jit(solution)/shard_map/ppermute | solution.py:588
  65.8 0.1 collective-permute-done
  65.9 0.1 multiply_convert_fusion
  66.0 11.2 %all_to_all.22 = bf16[8,16,768]{2,1,0:T(8,128)(2,1)S(1)} all-to-all(bf16[8,16,768]{2,1,0:T(8,128)(2,1)S(1)} %broadcast_in_dim.23), channel_id=1, replica_groups={{0,8,16,24,32,40,48,56},{64,72,80,88,96,104,112,120},{128,136,144,152,1..., dimensions={0} | all-to-all | bytes 393216 | tf_op jit(solution)/shard_map/all_to_all | solution.py:582
  77.3 0.9 collective-permute-start.3
  78.2 3.0 %collective-permute-start.4 = (bf16[128,768]{1,0:T(8,128)(2,1)S(1)}, bf16[128,768]{1,0:T(8,128)(2,1)S(1)}, u32[]{:S(2)}, u32[]{:S(2)}) collective-permute-start(bf16[128,768]{1,0:T(8,128)(2,1)S(1)} %bitcast.28), channel_id=1, source_target_pairs={{0,4},{1,5},{2,6},{3,7},{4,0},{5,1},{6,2},{7,3},{8,12},{9,13},{10,... | collective-permute-start | bytes 589832 | tf_op jit(solution)/shard_map/ppermute | solution.py:588
  81.2 0.0 collective-permute-start.5
  81.2 2.6 %copy-done.1 = bf16[8,1792,128]{2,1,0:T(8,128)(2,1)S(1)} copy-done((bf16[8,1792,128]{2,1,0:T(8,128)(2,1)S(1)}, bf16[8,1792,128]{2,1,0:T(8,128)(2,1)}, u32[]{:S(2)}) %copy-start.1) | copy-done | bytes 3670040
  83.8 11.5 %shard_map.132 = (bf16[768,2304]{1,0:T(8,128)(2,1)S(1)}, bf16[384,2304]{1,0:T(8,128)(2,1)S(1)}, bf16[2304,384]{1,0:T(8,128)(2,1)S(1)}, bf16[128,768]{1,0:T(8,128)(2,1)S(1)}) custom-call(s32[1]{0:T(128)} %bitcast.7.dp, bf16[8,1792,128]{2,1,0:T(8,128)(2,1)S(1)} %copy-done.1, f32[2,768]{1,0:T(2,128)S(1)} %copy-done.7, bf16[768,3072]{1,0:T(8,128)(2,1)} %bitcast.17, ...), custom_call_target="tpu_custom_call" | custom-call | flops 1358954496 | bytes 12000000 | tf_op jit(solution)/shard_map/pallas_call | solution.py:432
  95.4 0.0 collective-permute-done.3.b
  95.4 0.0 collective-permute-done.4.c
  95.4 0.0 collective-permute-done.5.d
  95.4 0.1 shard_map.133.near
  95.5 5.9 %collective-permute-start.6 = (bf16[512,768]{1,0:T(8,128)(2,1)S(1)}, bf16[512,768]{1,0:T(8,128)(2,1)S(1)}, u32[]{:S(2)}, u32[]{:S(2)}) collective-permute-start(bf16[512,768]{1,0:T(8,128)(2,1)S(1)} %shard_map.133.near), channel_id=1, source_target_pairs={{0,1},{1,0},{2,3},{3,2},{4,5},{5,4},{6,7},{7,6},{8,9},{9,8},{10,11... | collective-permute-start | bytes 2359304 | tf_op jit(solution)/shard_map/ppermute | solution.py:588
  103.3 0.1 pad_maximum_fusion.scalars
  103.3 0.0 collective-permute-done.6.far
  103.4 2.0 %shard_map.134.grads = f32[128,768]{1,0:T(8,128)S(1)} custom-call(f32[3]{0:T(128)S(1)} %pad_maximum_fusion.scalars, bf16[512,768]{1,0:T(8,128)(2,1)S(1)} %shard_map.133.near, bf16[512,768]{1,0:T(8,128)(2,1)S(1)} %collective-permute-done.6.far, f32[2,768]{1,0:T(2,128)S(1)} %copy-done.7), custom_call_target="tpu_custom_call" | custom-call | flops 301989888 | bytes 3000000 | tf_op jit(solution)/shard_map/pallas_call | solution.py:331
  105.3 0.0 slice-done
  105.4 0.0 slice-done.1
  105.4 0.0 copy-start
  105.4 2.4 %copy-done = bf16[1,3072,768]{2,1,0:T(8,128)(2,1)S(1)} copy-done((bf16[1,3072,768]{2,1,0:T(8,128)(2,1)S(1)}, bf16[1,3072,768]{2,1,0:T(8,128)(2,1)}, u32[]{:S(2)}) %copy-start) | copy-done | bytes 4718616
  107.7 5.8 %shard_map.135 = (bf16[1792,128]{1,0:T(8,128)(2,1)}, f32[8,128]{1,0:T(8,128)S(1)}) custom-call(bf16[304,768]{1,0:T(8,128)(2,1)} %get-tuple-element.22.bundle, bf16[288,256]{1,0:T(8,128)(2,1)S(1)} %get-tuple-element.23.hot, bf16[288,768]{1,0:T(8,128)(2,1)S(1)} %get-tuple-element.24.scaled_in, f32[128,768]{1,0:T(8,128)S(1)} %shard_map.134.grads, ...), custom_call_target="tpu_custom_call" | custom-call | flops 2717908992 | bytes 11206656 | tf_op jit(solution)/shard_map/pallas_call | solution.py:379
  113.6 0.0 copy-done.2
  113.6 0.0 copy-done.9
  113.6 0.0 copy-done.4
  113.6 0.0 copy-start.13
  113.6 4.1 %all-to-all-start.3 = ((bf16[32,56,128]{2,1,0:T(8,128)(2,1)}), bf16[32,56,128]{2,1,0:T(8,128)(2,1)S(1)}, u32[]{:S(2)}, u32[]{:S(2)}) async-start(bf16[32,56,128]{2,1,0:T(8,128)(2,1)} %bitcast.11), calls=%async_computation.3 | async-start | bytes 917504 | tf_op jit(solution)/shard_map/all_to_all | solution.py:577
  117.7 0.0 all-gather.6.cloned.1.call-done
  117.8 0.0 copy-done.13
  117.8 0.0 copy-start.5
  117.8 16.1 %shard_map.136 = (bf16[768,384]{1,0:T(8,128)(2,1)}, bf16[384,768]{1,0:T(8,128)(2,1)}, f32[8,128]{1,0:T(8,128)}) custom-call(s32[1]{0:T(128)} %bitcast.7.dp, f32[3]{0:T(128)} %copy-done.9, bf16[512,768]{1,0:T(8,128)(2,1)} %copy-done.2, bf16[512,768]{1,0:T(8,128)(2,1)} %copy-done.4, f32[2,768]{1,0:T(2,128)} %get-tuple-element.21.gains, ...), custom_call_target="tpu_custom_call" | custom-call | flops 6090129408 | bytes 15000000 | tf_op jit(solution)/shard_map/pallas_call | solution.py:513
  133.9 0.0 all-to-all-done.3
  133.9 0.7 copy-done.8
  134.6 1.1 shard_map.137
  (23 shorter events, 0.1 us)
Async XLA Ops:
  7.2 74.0 %all-gather.4.cloned.1.call-start = ((), (), s32[]{:S(2)}) async-start(), calls=%async_computation.4 | async-start | bytes 4128768 | tf_op jit(solution)/shard_map/all_gather | solution.py:617
  34.3 83.4 %all-gather.6.cloned.1.call-start = ((), (), s32[]{:S(2)}) async-start(), calls=%async_computation.5 | async-start | bytes 4202496 | tf_op jit(solution)/shard_map/all_gather | solution.py:619
  34.4 1.0 copy-start.3
  35.4 0.7 copy-start.6
  36.1 45.1 %copy-start.7 = (f32[2,768]{1,0:T(2,128)S(1)}, f32[2,768]{1,0:T(2,128)}, u32[]{:S(2)}) copy-start(f32[2,768]{1,0:T(2,128)} %get-tuple-element.21.gains) | copy-start | bytes 18436
  59.6 4.6 %collective-permute-start.1 = (f32[16,768]{1,0:T(8,128)S(1)}, f32[16,768]{1,0:T(8,128)S(1)}, u32[]{:S(2)}, u32[]{:S(2)}) collective-permute-start(f32[16,768]{1,0:T(8,128)S(1)} %convert_reduce_fusion), channel_id=1, source_target_pairs={{0,128},{8,136},{16,144},{24,152},{32,160},{40,168},{48,176},{56,1... | collective-permute-start | bytes 147464 | tf_op jit(solution)/shard_map/ppermute | solution.py:588
  61.3 4.6 %collective-permute-start.2 = (f32[16,768]{1,0:T(8,128)S(1)}, f32[16,768]{1,0:T(8,128)S(1)}, u32[]{:S(2)}, u32[]{:S(2)}) collective-permute-start(f32[16,768]{1,0:T(8,128)S(1)} %convert_reduce_fusion), channel_id=1, source_target_pairs={{0,192},{8,200},{16,208},{24,216},{32,224},{40,232},{48,240},{56,2... | collective-permute-start | bytes 147464 | tf_op jit(solution)/shard_map/ppermute | solution.py:588
  62.8 3.2 %collective-permute-start = (f32[16,768]{1,0:T(8,128)S(1)}, f32[16,768]{1,0:T(8,128)S(1)}, u32[]{:S(2)}, u32[]{:S(2)}) collective-permute-start(f32[16,768]{1,0:T(8,128)S(1)} %convert_reduce_fusion), channel_id=1, source_target_pairs={{0,64},{8,72},{16,80},{24,88},{32,96},{40,104},{48,112},{56,120},{... | collective-permute-start | bytes 147464 | tf_op jit(solution)/shard_map/ppermute | solution.py:588
  77.3 18.1 %collective-permute-start.3 = (bf16[128,768]{1,0:T(8,128)(2,1)S(1)}, bf16[128,768]{1,0:T(8,128)(2,1)S(1)}, u32[]{:S(2)}, u32[]{:S(2)}) collective-permute-start(bf16[128,768]{1,0:T(8,128)(2,1)S(1)} %bitcast.27), channel_id=1, source_target_pairs={{0,2},{1,3},{2,0},{3,1},{4,6},{5,7},{6,4},{7,5},{8,10},{9,11},{10,... | collective-permute-start | bytes 589832 | tf_op jit(solution)/shard_map/ppermute | solution.py:588
  78.2 17.2 %collective-permute-start.4 = (bf16[128,768]{1,0:T(8,128)(2,1)S(1)}, bf16[128,768]{1,0:T(8,128)(2,1)S(1)}, u32[]{:S(2)}, u32[]{:S(2)}) collective-permute-start(bf16[128,768]{1,0:T(8,128)(2,1)S(1)} %bitcast.28), channel_id=1, source_target_pairs={{0,4},{1,5},{2,6},{3,7},{4,0},{5,1},{6,2},{7,3},{8,12},{9,13},{10,... | collective-permute-start | bytes 589832 | tf_op jit(solution)/shard_map/ppermute | solution.py:588
  81.2 14.2 %collective-permute-start.5 = (bf16[128,768]{1,0:T(8,128)(2,1)S(1)}, bf16[128,768]{1,0:T(8,128)(2,1)S(1)}, u32[]{:S(2)}, u32[]{:S(2)}) collective-permute-start(bf16[128,768]{1,0:T(8,128)(2,1)S(1)} %bitcast.29), channel_id=1, source_target_pairs={{0,6},{1,7},{2,4},{3,5},{4,2},{5,3},{6,0},{7,1},{8,14},{9,15},{10,... | collective-permute-start | bytes 589832 | tf_op jit(solution)/shard_map/ppermute | solution.py:588
  81.2 24.1 %slice-start = ((s8[4718592]{0:T(1024)(128)(4,1)}), s8[4194304]{0:T(1024)(128)(4,1)S(1)}, s32[]{:S(2)}) async-start(s8[4718592]{0:T(1024)(128)(4,1)} %bitcast.18), calls=%async_computation.6 | async-start | bytes 8388608
  81.2 2.6 %copy-start.1 = (bf16[8,1792,128]{2,1,0:T(8,128)(2,1)S(1)}, bf16[8,1792,128]{2,1,0:T(8,128)(2,1)}, u32[]{:S(2)}) copy-start(bf16[8,1792,128]{2,1,0:T(8,128)(2,1)} %all-gather.4.cloned.1.call-done.arr) | copy-start | bytes 11010052
  83.8 21.6 %slice-start.1 = ((s8[4718592]{0:T(1024)(128)(4,1)}), s8[524288]{0:T(1024)(128)(4,1)S(1)}, s32[]{:S(2)}) async-start(s8[4718592]{0:T(1024)(128)(4,1)} %bitcast.18), calls=%async_computation.7 | async-start | bytes 1048576
  95.3 18.2 %copy-start.10 = (bf16[768,2304]{1,0:T(8,128)(2,1)}, bf16[768,2304]{1,0:T(8,128)(2,1)S(1)}, u32[]{:S(2)}) copy-start(bf16[768,2304]{1,0:T(8,128)(2,1)S(1)} %get-tuple-element.32.normed_t) | copy-start | bytes 10616836
  95.3 18.2 %copy-start.11 = (bf16[384,2304]{1,0:T(8,128)(2,1)}, bf16[384,2304]{1,0:T(8,128)(2,1)S(1)}, u32[]{:S(2)}) copy-start(bf16[384,2304]{1,0:T(8,128)(2,1)S(1)} %get-tuple-element.33.hidden_t) | copy-start | bytes 5308420
  95.4 18.2 %copy-start.12 = (bf16[2304,384]{1,0:T(8,128)(2,1)}, bf16[2304,384]{1,0:T(8,128)(2,1)S(1)}, u32[]{:S(2)}) copy-start(bf16[2304,384]{1,0:T(8,128)(2,1)S(1)} %get-tuple-element.30.slope) | copy-start | bytes 5308420
  95.5 18.1 %copy-start.2 = (bf16[512,768]{1,0:T(8,128)(2,1)}, bf16[512,768]{1,0:T(8,128)(2,1)S(1)}, u32[]{:S(2)}) copy-start(bf16[512,768]{1,0:T(8,128)(2,1)S(1)} %shard_map.133.near) | copy-start | bytes 2359300
  95.5 7.9 %collective-permute-start.6 = (bf16[512,768]{1,0:T(8,128)(2,1)S(1)}, bf16[512,768]{1,0:T(8,128)(2,1)S(1)}, u32[]{:S(2)}, u32[]{:S(2)}) collective-permute-start(bf16[512,768]{1,0:T(8,128)(2,1)S(1)} %shard_map.133.near), channel_id=1, source_target_pairs={{0,1},{1,0},{2,3},{3,2},{4,5},{5,4},{6,7},{7,6},{8,9},{9,8},{10,11... | collective-permute-start | bytes 2359304 | tf_op jit(solution)/shard_map/ppermute | solution.py:588
  103.3 10.2 %copy-start.9 = (f32[3]{0:T(128)}, f32[3]{0:T(128)S(1)}, u32[]{:S(2)}) copy-start(f32[3]{0:T(128)S(1)} %pad_maximum_fusion.scalars) | copy-start | bytes 40
  103.4 10.3 %copy-start.4 = (bf16[512,768]{1,0:T(8,128)(2,1)}, bf16[512,768]{1,0:T(8,128)(2,1)S(1)}, u32[]{:S(2)}) copy-start(bf16[512,768]{1,0:T(8,128)(2,1)S(1)} %collective-permute-done.6.far) | copy-start | bytes 2359300
  105.4 2.4 %copy-start = (bf16[1,3072,768]{2,1,0:T(8,128)(2,1)S(1)}, bf16[1,3072,768]{2,1,0:T(8,128)(2,1)}, u32[]{:S(2)}) copy-start(bf16[1,3072,768]{2,1,0:T(8,128)(2,1)} %param.18) | copy-start | bytes 14155780
  113.6 4.2 %copy-start.13 = (f32[8,128]{1,0:T(8,128)}, f32[8,128]{1,0:T(8,128)S(1)}, u32[]{:S(2)}) copy-start(f32[8,128]{1,0:T(8,128)S(1)} %get-tuple-element.31._) | copy-start | bytes 12292
  113.6 20.3 %all-to-all-start.3 = ((bf16[32,56,128]{2,1,0:T(8,128)(2,1)}), bf16[32,56,128]{2,1,0:T(8,128)(2,1)S(1)}, u32[]{:S(2)}, u32[]{:S(2)}) async-start(bf16[32,56,128]{2,1,0:T(8,128)(2,1)} %bitcast.11), calls=%async_computation.3 | async-start | bytes 917504 | tf_op jit(solution)/shard_map/all_to_all | solution.py:577
  117.8 16.1 %copy-start.5 = (f32[132,1]{1,0:T(8,128)S(1)}, f32[132,1]{1,0:T(8,128)}, u32[]{:S(2)}) copy-start(f32[132,1]{1,0:T(8,128)} %get-tuple-element.29.slot) | copy-start | bytes 1588
  133.9 0.7 copy-start.8
Sparse Core Ops, SparseCore 0:
  34.5 33.0 all-gather.3
  69.9 39.7 all-gather.5
where the time goes:
time: 143 us
  blocking collectives  50.4 us (35%)
  Pallas kernels  48 us (34%)
  starting transfers between devices  17.2 us (12%)
  between operations  16.2 us (11%)
  local copies, waits for them, and re-layouts  7.37 us (5%)
  waiting for transfers between devices  3.22 us (2%)
    all_to_all x2, blocking collectives, along_z(): lax.all_to_all(values, 'expert', split_axis=0, concat_axis=0, tiled=True,...  25.5 us
    all_to_all x1, blocking collectives, to_experts(): lax.all_to_all(slabs, 'expert', split_axis=0, concat_axis=0, tiled=True)  24.9 us
    pallas_call x1, Pallas kernels, weight_grads(): pl.pallas_call(weights_kernel, grid_spec=pltpu.PrefetchScalarGridSpec(num...  16.1 us
    ppermute x7, starting transfers between devices, swap(): return lax.ppermute(values, axis, [(i, i ^ by) for i in range(size)])  13 us
    pallas_call x1, Pallas kernels, hidden_slice(): pl.pallas_call(slice_kernel, grid_spec=pltpu.PrefetchScalarGridSpec(num_s...  11.5 us
    pallas_call x1, Pallas kernels, forward(): pl.pallas_call(forward_kernel, in_specs=[VM, VM, IN_HBM, IN_HBM], out_spe...  9.17 us
    unnamed x32, local copies, waits for them, and re-layouts  7.35 us
    pallas_call x1, Pallas kernels, backward(): pl.pallas_call(backward_kernel, in_specs=[VM] * 8, out_specs=(VM, VM), ou...  5.83 us
  transfers between devices with their start and end apart: 10, of which 3 were waited for; matrix products, arithmetic and copies ran while one was open for 0% of the time, Pallas kernels for 31%

commit v1 on v0

--- a/solution.py
+++ b/solution.py
@@ -291,7 +291,7 @@
     return (inv * share) * (grad - u * jnp.sum(u * grad, axis=1, keepdims=True)) * gain
 
 
-def own_loss_kernel(scalars, near, far, gains, own, unit, inverse, img, txt):
+def own_loss(scalars, near, far, gains, unit, inverse, img, txt):
     load_units(near, far, unit, inverse, img, txt, 1)
 
     def side(mine, others):
@@ -299,7 +299,7 @@
         both = dot(jnp.concatenate([hi, low], axis=0), others[...])
         return both[:HALF] + both[HALF:]
 
-    own[...] = pool_grads(side(img, txt), side(txt, img), unit[...], inverse[...], gains[1:2, :])
+    return pool_grads(side(img, txt), side(txt, img), unit[...], inverse[...], gains[1:2, :])
 
 
 def all_loss(scalars, near, far, gains, every, unit, inverse, img, txt):
@@ -327,28 +327,13 @@
     )(*pieces)
 
 
-def own_loss(scalars, near, far, gains):
-    return pl.pallas_call(
-        own_loss_kernel,
-        in_specs=[pl.BlockSpec(memory_space=pltpu.SMEM)] + [VM] * 3,
-        out_specs=VM,
-        out_shape=jax.ShapeDtypeStruct((GROUP, D), F32),
-        scratch_shapes=[
-            pltpu.VMEM((GROUP, D), F32),
-            pltpu.VMEM((GROUP, 1), F32),
-            pltpu.VMEM((PAIRS, D), BF),
-            pltpu.VMEM((PAIRS, D), BF),
-        ],
-        compiler_params=params(24),
-        cost_estimate=cost(6 * GROUP * PAIRS * D, 3000000, GROUP * PAIRS),
-    )(scalars, near, far, gains)
-
-
 def backward_kernel(
-    bundle, hot, scaled_in, grads, gains, slope, w1, w2, out, mark,
-    scr, mixed, rows, acc,
+    scalars, near, far, gains, bundle, hot, scaled_in, slope, w1, w2, out, mark,
+    scr, mixed, rows, acc, unit, inverse, img, txt, w2v, sem,
 ):
-    hi, low = two(grads[...])
+    fetch = pltpu.make_async_copy(w2, w2v, sem)
+    fetch.start()
+    hi, low = two(own_loss(scalars, near, far, gains, unit, inverse, img, txt))
     mixed[...] = dot(hot[:, :GROUP], hi) + dot(hot[:, :GROUP], low)
 
     def column(at, n):
@@ -359,9 +344,10 @@
         grad = norm_back(mixed[at, :], bundle[at, :].astype(F32), column(at, 0))
         mixed[at, :] = grad
         rows[at, :] = (column(at, 2) * grad).astype(BF)
+    fetch.wait()
     for i in range(H // HB):
         at = slice(i * HB, (i + 1) * HB)
-        hidden = (dot(rows[...], w2[at, :], 1, 1) * slope[:, at].astype(F32)).astype(BF)
+        hidden = (dot(rows[...], w2v[at, :], 1, 1) * slope[:, at].astype(F32)).astype(BF)
         term = dot(hidden, w1[:, at], 1, 1)
         acc[...] = term if i == 0 else acc[...] + term
     for j in range(CAP):
@@ -375,10 +361,10 @@
     mark[...] = jnp.zeros_like(mark)
 
 
-def backward(bundle, hot, scaled_in, grads, gains, slope, w1, w2):
+def backward(scalars, near, far, gains, bundle, hot, scaled_in, slope, w1, w2):
     return pl.pallas_call(
         backward_kernel,
-        in_specs=[VM] * 8,
+        in_specs=[pl.BlockSpec(memory_space=pltpu.SMEM)] + [VM] * 8 + [IN_HBM],
         out_specs=(VM, VM),
         out_shape=(jax.ShapeDtypeStruct((PACKED, LANES), BF), MARK),
         scratch_shapes=[
@@ -386,10 +372,16 @@
             pltpu.VMEM((ROWS, D), F32),
             pltpu.VMEM((ROWS, D), BF),
             pltpu.VMEM((ROWS, D), F32),
+            pltpu.VMEM((GROUP, D), F32),
+            pltpu.VMEM((GROUP, 1), F32),
+            pltpu.VMEM((PAIRS, D), BF),
+            pltpu.VMEM((PAIRS, D), BF),
+            pltpu.VMEM((H, D), BF),
+            pltpu.SemaphoreType.DMA,
         ],
-        compiler_params=params(24),
-        cost_estimate=cost(4 * ROWS * D * H, 4 * D * H + 2 * ROWS * H),
-    )(bundle, hot, scaled_in, grads, gains, slope, w1, w2)
+        compiler_params=params(44),
+        cost_estimate=cost(4 * ROWS * D * H + 6 * GROUP * PAIRS * D, 4 * D * H + 2 * ROWS * H),
+    )(scalars, near, far, gains, bundle, hot, scaled_in, slope, w1, w2)
 
 
 def slice_kernel(
@@ -461,7 +453,7 @@
             jax.ShapeDtypeStruct((ALL, HS), BF),
             jax.ShapeDtypeStruct((GROUP, D), BF),
         ),
-        compiler_params=params(40),
+        compiler_params=params(50),
         cost_estimate=cost(2 * ALL * D * HS, 12000000, 2 * ALL * HS),
     )(dp, arrs, gains, w1, pooled)
 
@@ -629,8 +621,7 @@
     far = swap(near, "dp", DP, 1)
 
     scalars = jnp.concatenate([sharpness_factor, similarity_shift_term, objective_adjoint_factor])
-    own = own_loss(scalars, near, far, gains)
-    packed, mark = backward(bundle, hot, scaled_in, own, gains, slope, w1, w2)
+    packed, mark = backward(scalars, near, far, gains, bundle, hot, scaled_in, slope, w1, w2)
     returned = to_experts(packed)
     grad_in, grad_out, mark = weight_grads(
         dp, scalars, near, far, gains, bundles, grads, mark, normed_t, hidden_t, w2

time: 143 us -> 144 us (level)
  Pallas kernels: 48 us -> 53.6 us
  local copies, waits for them, and re-layouts: 7.37 us -> 2.43 us
    unnamed x32 -> x26, local copies, waits for them, and re-layouts: 7.35 us -> 2.41 us
    pallas_call x1, Pallas kernels: 11.5 us -> 15.3 us  [hidden_slice(): pl.pallas_call(slice_kernel, grid_spec=pltpu.PrefetchScalarGridSpec(num_s...]
    pallas_call x2 -> x1, Pallas kernels: 7.81 us -> 9.67 us  [backward(): pl.pallas_call(backward_kernel, in_specs=[pl.BlockSpec(memory_space=pltpu...]
  transfers between devices with their start and end apart: 10 -> 10, of which waited for: 3 -> 3; matrix products, arithmetic and copies ran while one was open for 0% -> 0% of each run, Pallas kernels for 31% -> 35%
where the time goes in v1:
time: 144 us; the launch traced here: 143 us
  Pallas kernels  53.6 us (37%)
  blocking collectives  50.4 us (35%)
  starting transfers between devices  17.1 us (12%)
  between operations  16.2 us (11%)
  waiting for transfers between devices  3.22 us (2%)
  local copies, waits for them, and re-layouts  2.43 us (2%)
    all_to_all x2, blocking collectives, along_z(): lax.all_to_all(values, 'expert', split_axis=0, concat_axis=0, tiled=True,...  25.5 us
    all_to_all x1, blocking collectives, to_experts(): lax.all_to_all(slabs, 'expert', split_axis=0, concat_axis=0, tiled=True)  24.9 us
    pallas_call x1, Pallas kernels, weight_grads(): pl.pallas_call(weights_kernel, grid_spec=pltpu.PrefetchScalarGridSpec(num...  16.1 us
    pallas_call x1, Pallas kernels, hidden_slice(): pl.pallas_call(slice_kernel, grid_spec=pltpu.PrefetchScalarGridSpec(num_s...  15.3 us
    ppermute x7, starting transfers between devices, swap(): return lax.ppermute(values, axis, [(i, i ^ by) for i in range(size)])  12.9 us
    pallas_call x1, Pallas kernels, backward(): pl.pallas_call(backward_kernel, in_specs=[pl.BlockSpec(memory_space=pltpu...  9.67 us
    pallas_call x1, Pallas kernels, forward(): pl.pallas_call(forward_kernel, in_specs=[VM, VM, IN_HBM, IN_HBM], out_spe...  9.17 us
    all_to_all x1, starting transfers between devices, to_experts(): lax.all_to_all(slabs, 'expert', split_axis=0, concat_axis=0, tiled=True)  4.12 us
  transfers between devices with their start and end apart: 10, of which 3 were waited for; matrix products, arithmetic and copies ran while one was open for 0% of the time, Pallas kernels for 35%

profile of v1, /device:TPU:1, one launch (start us, length us, event | category | flops | bytes accessed | tf_op | source)
XLA Modules:
  0.0 143.1 jit_solution(4813297516951724686)
XLA Ops:
  7.2 0.0 all-gather.4.cloned.1.call-start
  7.2 2.2 %shard_map.130 = (bf16[1792,128]{1,0:T(8,128)(2,1)}, f32[132,1]{1,0:T(8,128)}, f32[2,768]{1,0:T(2,128)}) custom-call(bf16[132,768]{1,0:T(8,128)(2,1)} %x.1, s32[1,132]{1,0:T(1,128)} %bitcast.33, s32[1,132]{1,0:T(1,128)} %bitcast.34, f32[1,132]{1,0:T(1,128)} %bitcast.35, f32[768]{0:T(1024)} %gain_in.1, f32[768]{0:T(1024)} %gain_out.1), custom_call_target="tpu_custom_call" | custom-call | flops 58392576 | bytes 700000 | tf_op jit(solution)/shard_map/pallas_call | solution.py:159
  9.4 24.9 %all_to_all.20 = bf16[32,56,128]{2,1,0:T(8,128)(2,1)} all-to-all(bf16[32,56,128]{2,1,0:T(8,128)(2,1)} %bitcast.32), channel_id=1, replica_groups=mesh['expert'=32,'dp'=8] {'expert'}, dimensions={0} | all-to-all | bytes 917504 | tf_op jit(solution)/shard_map/all_to_all | solution.py:569
  34.3 0.0 all-gather.4.cloned.1.call-update
  34.3 0.0 all-gather.6.cloned.1.call-start
  34.4 0.0 copy-start.1
  34.4 1.0 copy-done.1
  35.4 0.7 copy-done.4
  36.1 9.2 %shard_map.131 = (bf16[128,768]{1,0:T(8,128)(2,1)S(1)}, bf16[304,768]{1,0:T(8,128)(2,1)}, bf16[288,3072]{1,0:T(8,128)(2,1)S(1)}, bf16[288,256]{1,0:T(8,128)(2,1)S(1)}, bf16[288,768]{1,0:T(8,128)(2,1)S(1)}) custom-call(bf16[1792,128]{1,0:T(8,128)(2,1)S(1)} %bitcast.22, f32[2,768]{1,0:T(2,128)S(1)} %copy-done.4, bf16[768,3072]{1,0:T(8,128)(2,1)} %bitcast.16, ...), custom_call_target="tpu_custom_call" | custom-call | flops 2717908992 | bytes 9437184 | tf_op jit(solution)/shard_map/pallas_call | solution.py:236
  45.3 0.0 all-gather.6.cloned.1.call-update
  45.3 14.2 %all_to_all.21 = bf16[8,16,768]{2,1,0:T(8,128)(2,1)S(1)} all-to-all(bf16[8,16,768]{2,1,0:T(8,128)(2,1)S(1)} %bitcast.28), channel_id=1, replica_groups={{0,8,16,24,32,40,48,56},{64,72,80,88,96,104,112,120},{128,136,144,152,1..., dimensions={0} | all-to-all | bytes 393216 | tf_op jit(solution)/shard_map/all_to_all | solution.py:574
  59.6 1.7 %collective-permute-start.1 = (f32[16,768]{1,0:T(8,128)S(1)}, f32[16,768]{1,0:T(8,128)S(1)}, u32[]{:S(2)}, u32[]{:S(2)}) collective-permute-start(f32[16,768]{1,0:T(8,128)S(1)} %convert_reduce_fusion), channel_id=1, source_target_pairs={{0,128},{8,136},{16,144},{24,152},{32,160},{40,168},{48,176},{56,1... | collective-permute-start | bytes 147464 | tf_op jit(solution)/shard_map/ppermute | solution.py:580
  61.3 1.5 %collective-permute-start.2 = (f32[16,768]{1,0:T(8,128)S(1)}, f32[16,768]{1,0:T(8,128)S(1)}, u32[]{:S(2)}, u32[]{:S(2)}) collective-permute-start(f32[16,768]{1,0:T(8,128)S(1)} %convert_reduce_fusion), channel_id=1, source_target_pairs={{0,192},{8,200},{16,208},{24,216},{32,224},{40,232},{48,240},{56,2... | collective-permute-start | bytes 147464 | tf_op jit(solution)/shard_map/ppermute | solution.py:580
  62.8 0.0 collective-permute-start
  62.8 1.4 collective-permute-done.1
  64.2 1.7 %collective-permute-done.2 = f32[16,768]{1,0:T(8,128)S(1)} collective-permute-done((f32[16,768]{1,0:T(8,128)S(1)}, f32[16,768]{1,0:T(8,128)S(1)}, u32[]{:S(2)}, u32[]{:S(2)}) %collective-permute-start.2) | collective-permute-done | bytes 49184 | tf_op jit(solution)/shard_map/ppermute | solution.py:580
  65.8 0.1 collective-permute-done
  65.9 0.1 multiply_convert_fusion
  66.0 11.2 %all_to_all.22 = bf16[8,16,768]{2,1,0:T(8,128)(2,1)S(1)} all-to-all(bf16[8,16,768]{2,1,0:T(8,128)(2,1)S(1)} %broadcast_in_dim.23), channel_id=1, replica_groups={{0,8,16,24,32,40,48,56},{64,72,80,88,96,104,112,120},{128,136,144,152,1..., dimensions={0} | all-to-all | bytes 393216 | tf_op jit(solution)/shard_map/all_to_all | solution.py:574
  77.3 0.9 collective-permute-start.3
  78.2 3.0 %collective-permute-start.4 = (bf16[128,768]{1,0:T(8,128)(2,1)S(1)}, bf16[128,768]{1,0:T(8,128)(2,1)S(1)}, u32[]{:S(2)}, u32[]{:S(2)}) collective-permute-start(bf16[128,768]{1,0:T(8,128)(2,1)S(1)} %bitcast.25), channel_id=1, source_target_pairs={{0,4},{1,5},{2,6},{3,7},{4,0},{5,1},{6,2},{7,3},{8,12},{9,13},{10,... | collective-permute-start | bytes 589832 | tf_op jit(solution)/shard_map/ppermute | solution.py:580
  81.2 0.0 collective-permute-start.5
  81.2 0.0 copy-done.5
  81.2 0.0 slice-start.1
  81.2 15.3 %shard_map.132 = (bf16[768,2304]{1,0:T(8,128)(2,1)}, bf16[384,2304]{1,0:T(8,128)(2,1)S(1)}, bf16[2304,384]{1,0:T(8,128)(2,1)S(1)}, bf16[128,768]{1,0:T(8,128)(2,1)S(1)}) custom-call(s32[1]{0:T(128)} %bitcast.dp, bf16[8,1792,128]{2,1,0:T(8,128)(2,1)} %all-gather.4.cloned.1.call-done.arr, f32[2,768]{1,0:T(2,128)S(1)} %copy-done.5, bf16[768,3072]{1,0:T(8,128)(2,1)} %bitcast.17, ...), custom_call_target="tpu_custom_call" | custom-call | flops 1358954496 | bytes 12000000 | tf_op jit(solution)/shard_map/pallas_call | solution.py:424
  96.6 0.0 copy-start.8
  96.6 0.0 copy-start.9
  96.6 0.0 collective-permute-done.3.b
  96.6 0.0 collective-permute-done.4.c
  96.6 0.0 collective-permute-done.5.d
  96.6 0.1 shard_map.133.near
  96.7 0.0 copy-start
  96.7 5.7 %collective-permute-start.6 = (bf16[512,768]{1,0:T(8,128)(2,1)S(1)}, bf16[512,768]{1,0:T(8,128)(2,1)S(1)}, u32[]{:S(2)}, u32[]{:S(2)}) collective-permute-start(bf16[512,768]{1,0:T(8,128)(2,1)S(1)} %shard_map.133.near), channel_id=1, source_target_pairs={{0,1},{1,0},{2,3},{3,2},{4,5},{5,4},{6,7},{7,6},{8,9},{9,8},{10,11... | collective-permute-start | bytes 2359304 | tf_op jit(solution)/shard_map/ppermute | solution.py:580
  104.3 0.1 pad_maximum_fusion.scalars
  104.4 0.0 collective-permute-done.6.far
  104.4 0.0 slice-done
  104.4 0.0 slice-done.1
  104.5 9.7 %shard_map.134 = (bf16[1792,128]{1,0:T(8,128)(2,1)}, f32[8,128]{1,0:T(8,128)S(1)}) custom-call(f32[3]{0:T(128)S(1)} %pad_maximum_fusion.scalars, bf16[512,768]{1,0:T(8,128)(2,1)S(1)} %shard_map.133.near, bf16[512,768]{1,0:T(8,128)(2,1)S(1)} %collective-permute-done.6.far, f32[2,768]{1,0:T(2,128)S(1)} %copy-done.5, ...), custom_call_target="tpu_custom_call" | custom-call | flops 3019898880 | bytes 11206656 | tf_op jit(solution)/shard_map/pallas_call | solution.py:365
  114.1 0.0 copy-done.8
  114.2 0.0 copy-done.9
  114.2 4.1 %all-to-all-start.3 = ((bf16[32,56,128]{2,1,0:T(8,128)(2,1)}), bf16[32,56,128]{2,1,0:T(8,128)(2,1)S(1)}, u32[]{:S(2)}, u32[]{:S(2)}) async-start(bf16[32,56,128]{2,1,0:T(8,128)(2,1)} %bitcast.11), calls=%async_computation.3 | async-start | bytes 917504 | tf_op jit(solution)/shard_map/all_to_all | solution.py:569
  118.3 0.0 all-gather.6.cloned.1.call-done
  118.4 0.0 copy-done.10
  118.4 0.0 copy-start.3
  118.4 16.1 %shard_map.135 = (bf16[768,384]{1,0:T(8,128)(2,1)}, bf16[384,768]{1,0:T(8,128)(2,1)}, f32[8,128]{1,0:T(8,128)}) custom-call(s32[1]{0:T(128)} %bitcast.dp, f32[3]{0:T(128)} %copy-done.7, bf16[512,768]{1,0:T(8,128)(2,1)} %copy-done, bf16[512,768]{1,0:T(8,128)(2,1)} %copy-done.2, f32[2,768]{1,0:T(2,128)} %get-tuple-element.21.gains, ...), custom_call_target="tpu_custom_call" | custom-call | flops 6090129408 | bytes 15000000 | tf_op jit(solution)/shard_map/pallas_call | solution.py:505
  134.5 0.0 all-to-all-done.3
  134.5 0.7 copy-done.6
  135.2 1.1 shard_map.136
  (16 shorter events, 0.1 us)
Async XLA Ops:
  7.2 74.0 %all-gather.4.cloned.1.call-start = ((), (), s32[]{:S(2)}) async-start(), calls=%async_computation.4 | async-start | bytes 4128768 | tf_op jit(solution)/shard_map/all_gather | solution.py:609
  34.3 84.0 %all-gather.6.cloned.1.call-start = ((), (), s32[]{:S(2)}) async-start(), calls=%async_computation.5 | async-start | bytes 4202496 | tf_op jit(solution)/shard_map/all_gather | solution.py:611
  34.4 1.0 copy-start.1
  35.4 0.7 copy-start.4
  36.1 45.1 %copy-start.5 = (f32[2,768]{1,0:T(2,128)S(1)}, f32[2,768]{1,0:T(2,128)}, u32[]{:S(2)}) copy-start(f32[2,768]{1,0:T(2,128)} %get-tuple-element.21.gains) | copy-start | bytes 18436
  59.6 4.6 %collective-permute-start.1 = (f32[16,768]{1,0:T(8,128)S(1)}, f32[16,768]{1,0:T(8,128)S(1)}, u32[]{:S(2)}, u32[]{:S(2)}) collective-permute-start(f32[16,768]{1,0:T(8,128)S(1)} %convert_reduce_fusion), channel_id=1, source_target_pairs={{0,128},{8,136},{16,144},{24,152},{32,160},{40,168},{48,176},{56,1... | collective-permute-start | bytes 147464 | tf_op jit(solution)/shard_map/ppermute | solution.py:580
  61.3 4.6 %collective-permute-start.2 = (f32[16,768]{1,0:T(8,128)S(1)}, f32[16,768]{1,0:T(8,128)S(1)}, u32[]{:S(2)}, u32[]{:S(2)}) collective-permute-start(f32[16,768]{1,0:T(8,128)S(1)} %convert_reduce_fusion), channel_id=1, source_target_pairs={{0,192},{8,200},{16,208},{24,216},{32,224},{40,232},{48,240},{56,2... | collective-permute-start | bytes 147464 | tf_op jit(solution)/shard_map/ppermute | solution.py:580
  62.8 3.2 %collective-permute-start = (f32[16,768]{1,0:T(8,128)S(1)}, f32[16,768]{1,0:T(8,128)S(1)}, u32[]{:S(2)}, u32[]{:S(2)}) collective-permute-start(f32[16,768]{1,0:T(8,128)S(1)} %convert_reduce_fusion), channel_id=1, source_target_pairs={{0,64},{8,72},{16,80},{24,88},{32,96},{40,104},{48,112},{56,120},{... | collective-permute-start | bytes 147464 | tf_op jit(solution)/shard_map/ppermute | solution.py:580
  77.3 19.3 %collective-permute-start.3 = (bf16[128,768]{1,0:T(8,128)(2,1)S(1)}, bf16[128,768]{1,0:T(8,128)(2,1)S(1)}, u32[]{:S(2)}, u32[]{:S(2)}) collective-permute-start(bf16[128,768]{1,0:T(8,128)(2,1)S(1)} %bitcast.24), channel_id=1, source_target_pairs={{0,2},{1,3},{2,0},{3,1},{4,6},{5,7},{6,4},{7,5},{8,10},{9,11},{10,... | collective-permute-start | bytes 589832 | tf_op jit(solution)/shard_map/ppermute | solution.py:580
  78.2 18.4 %collective-permute-start.4 = (bf16[128,768]{1,0:T(8,128)(2,1)S(1)}, bf16[128,768]{1,0:T(8,128)(2,1)S(1)}, u32[]{:S(2)}, u32[]{:S(2)}) collective-permute-start(bf16[128,768]{1,0:T(8,128)(2,1)S(1)} %bitcast.25), channel_id=1, source_target_pairs={{0,4},{1,5},{2,6},{3,7},{4,0},{5,1},{6,2},{7,3},{8,12},{9,13},{10,... | collective-permute-start | bytes 589832 | tf_op jit(solution)/shard_map/ppermute | solution.py:580
  81.2 15.4 %collective-permute-start.5 = (bf16[128,768]{1,0:T(8,128)(2,1)S(1)}, bf16[128,768]{1,0:T(8,128)(2,1)S(1)}, u32[]{:S(2)}, u32[]{:S(2)}) collective-permute-start(bf16[128,768]{1,0:T(8,128)(2,1)S(1)} %bitcast.26), channel_id=1, source_target_pairs={{0,6},{1,7},{2,4},{3,5},{4,2},{5,3},{6,0},{7,1},{8,14},{9,15},{10,... | collective-permute-start | bytes 589832 | tf_op jit(solution)/shard_map/ppermute | solution.py:580
  81.2 23.2 %slice-start = ((s8[4718592]{0:T(1024)(128)(4,1)}), s8[4194304]{0:T(1024)(128)(4,1)S(1)}, s32[]{:S(2)}) async-start(s8[4718592]{0:T(1024)(128)(4,1)} %bitcast.18), calls=%async_computation.6 | async-start | bytes 8388608
  81.2 23.2 %slice-start.1 = ((s8[4718592]{0:T(1024)(128)(4,1)}), s8[524288]{0:T(1024)(128)(4,1)S(1)}, s32[]{:S(2)}) async-start(s8[4718592]{0:T(1024)(128)(4,1)} %bitcast.18), calls=%async_computation.7 | async-start | bytes 1048576
  96.6 17.6 %copy-start.8 = (bf16[384,2304]{1,0:T(8,128)(2,1)}, bf16[384,2304]{1,0:T(8,128)(2,1)S(1)}, u32[]{:S(2)}) copy-start(bf16[384,2304]{1,0:T(8,128)(2,1)S(1)} %get-tuple-element.33.hidden_t) | copy-start | bytes 5308420
  96.6 17.6 %copy-start.9 = (bf16[2304,384]{1,0:T(8,128)(2,1)}, bf16[2304,384]{1,0:T(8,128)(2,1)S(1)}, u32[]{:S(2)}) copy-start(bf16[2304,384]{1,0:T(8,128)(2,1)S(1)} %get-tuple-element.30.slope) | copy-start | bytes 5308420
  96.7 17.5 %copy-start = (bf16[512,768]{1,0:T(8,128)(2,1)}, bf16[512,768]{1,0:T(8,128)(2,1)S(1)}, u32[]{:S(2)}) copy-start(bf16[512,768]{1,0:T(8,128)(2,1)S(1)} %shard_map.133.near) | copy-start | bytes 2359300
  96.7 7.8 %collective-permute-start.6 = (bf16[512,768]{1,0:T(8,128)(2,1)S(1)}, bf16[512,768]{1,0:T(8,128)(2,1)S(1)}, u32[]{:S(2)}, u32[]{:S(2)}) collective-permute-start(bf16[512,768]{1,0:T(8,128)(2,1)S(1)} %shard_map.133.near), channel_id=1, source_target_pairs={{0,1},{1,0},{2,3},{3,2},{4,5},{5,4},{6,7},{7,6},{8,9},{9,8},{10,11... | collective-permute-start | bytes 2359304 | tf_op jit(solution)/shard_map/ppermute | solution.py:580
  104.4 9.8 %copy-start.7 = (f32[3]{0:T(128)}, f32[3]{0:T(128)S(1)}, u32[]{:S(2)}) copy-start(f32[3]{0:T(128)S(1)} %pad_maximum_fusion.scalars) | copy-start | bytes 40
  104.4 9.8 %copy-start.2 = (bf16[512,768]{1,0:T(8,128)(2,1)}, bf16[512,768]{1,0:T(8,128)(2,1)S(1)}, u32[]{:S(2)}) copy-start(bf16[512,768]{1,0:T(8,128)(2,1)S(1)} %collective-permute-done.6.far) | copy-start | bytes 2359300
  114.2 4.2 %copy-start.10 = (f32[8,128]{1,0:T(8,128)}, f32[8,128]{1,0:T(8,128)S(1)}, u32[]{:S(2)}) copy-start(f32[8,128]{1,0:T(8,128)S(1)} %get-tuple-element.31._) | copy-start | bytes 12292
  114.2 20.3 %all-to-all-start.3 = ((bf16[32,56,128]{2,1,0:T(8,128)(2,1)}), bf16[32,56,128]{2,1,0:T(8,128)(2,1)S(1)}, u32[]{:S(2)}, u32[]{:S(2)}) async-start(bf16[32,56,128]{2,1,0:T(8,128)(2,1)} %bitcast.11), calls=%async_computation.3 | async-start | bytes 917504 | tf_op jit(solution)/shard_map/all_to_all | solution.py:569
  118.4 16.1 %copy-start.3 = (f32[132,1]{1,0:T(8,128)S(1)}, f32[132,1]{1,0:T(8,128)}, u32[]{:S(2)}) copy-start(f32[132,1]{1,0:T(8,128)} %get-tuple-element.29.slot) | copy-start | bytes 1588
  134.5 0.7 copy-start.6
Sparse Core Ops, SparseCore 0:
  34.5 33.0 all-gather.3
  69.9 39.7 all-gather.5

commit v2 on v1

--- a/solution.py
+++ b/solution.py
@@ -329,10 +329,8 @@
 
 def backward_kernel(
     scalars, near, far, gains, bundle, hot, scaled_in, slope, w1, w2, out, mark,
-    scr, mixed, rows, acc, unit, inverse, img, txt, w2v, sem,
+    scr, mixed, rows, acc, unit, inverse, img, txt,
 ):
-    fetch = pltpu.make_async_copy(w2, w2v, sem)
-    fetch.start()
     hi, low = two(own_loss(scalars, near, far, gains, unit, inverse, img, txt))
     mixed[...] = dot(hot[:, :GROUP], hi) + dot(hot[:, :GROUP], low)
 
@@ -344,10 +342,9 @@
         grad = norm_back(mixed[at, :], bundle[at, :].astype(F32), column(at, 0))
         mixed[at, :] = grad
         rows[at, :] = (column(at, 2) * grad).astype(BF)
-    fetch.wait()
     for i in range(H // HB):
         at = slice(i * HB, (i + 1) * HB)
-        hidden = (dot(rows[...], w2v[at, :], 1, 1) * slope[:, at].astype(F32)).astype(BF)
+        hidden = (dot(rows[...], w2[at, :], 1, 1) * slope[:, at].astype(F32)).astype(BF)
         term = dot(hidden, w1[:, at], 1, 1)
         acc[...] = term if i == 0 else acc[...] + term
     for j in range(CAP):
@@ -364,7 +361,7 @@
 def backward(scalars, near, far, gains, bundle, hot, scaled_in, slope, w1, w2):
     return pl.pallas_call(
         backward_kernel,
-        in_specs=[pl.BlockSpec(memory_space=pltpu.SMEM)] + [VM] * 8 + [IN_HBM],
+        in_specs=[pl.BlockSpec(memory_space=pltpu.SMEM)] + [VM] * 9,
         out_specs=(VM, VM),
         out_shape=(jax.ShapeDtypeStruct((PACKED, LANES), BF), MARK),
         scratch_shapes=[
@@ -376,10 +373,8 @@
             pltpu.VMEM((GROUP, 1), F32),
             pltpu.VMEM((PAIRS, D), BF),
             pltpu.VMEM((PAIRS, D), BF),
-            pltpu.VMEM((H, D), BF),
-            pltpu.SemaphoreType.DMA,
         ],
-        compiler_params=params(44),
+        compiler_params=params(24),
         cost_estimate=cost(4 * ROWS * D * H + 6 * GROUP * PAIRS * D, 4 * D * H + 2 * ROWS * H),
     )(scalars, near, far, gains, bundle, hot, scaled_in, slope, w1, w2)
 
@@ -453,7 +448,7 @@
             jax.ShapeDtypeStruct((ALL, HS), BF),
             jax.ShapeDtypeStruct((GROUP, D), BF),
         ),
-        compiler_params=params(50),
+        compiler_params=params(40),
         cost_estimate=cost(2 * ALL * D * HS, 12000000, 2 * ALL * HS),
     )(dp, arrs, gains, w1, pooled)
 

time: 144 us -> 140 us (0.972)
  Pallas kernels: 53.6 us -> 47.7 us
  local copies, waits for them, and re-layouts: 2.43 us -> 5 us
    pallas_call x1, Pallas kernels: 15.3 us -> 11.5 us  [hidden_slice(): pl.pallas_call(slice_kernel, grid_spec=pltpu.PrefetchScalarGridSpec(num_s...]
    unnamed x26 -> x32, local copies, waits for them, and re-layouts: 2.41 us -> 4.98 us
    pallas_call x1, Pallas kernels: 9.67 us -> 7.58 us  [backward(): pl.pallas_call(backward_kernel, in_specs=[pl.BlockSpec(memory_space=pltpu...]
  transfers between devices with their start and end apart: 10 -> 10, of which waited for: 3 -> 3; matrix products, arithmetic and copies ran while one was open for 0% -> 0% of each run, Pallas kernels for 35% -> 32%
where the time goes in v2:
time: 140 us
  blocking collectives  50.4 us (36%)
  Pallas kernels  47.7 us (34%)
  starting transfers between devices  17.2 us (12%)
  between operations  16.2 us (12%)
  local copies, waits for them, and re-layouts  5 us (4%)
  waiting for transfers between devices  3.22 us (2%)
    all_to_all x2, blocking collectives, along_z(): lax.all_to_all(values, 'expert', split_axis=0, concat_axis=0, tiled=True,...  25.5 us
    all_to_all x1, blocking collectives, to_experts(): lax.all_to_all(slabs, 'expert', split_axis=0, concat_axis=0, tiled=True)  24.9 us
    pallas_call x1, Pallas kernels, weight_grads(): pl.pallas_call(weights_kernel, grid_spec=pltpu.PrefetchScalarGridSpec(num...  16.1 us
    ppermute x7, starting transfers between devices, swap(): return lax.ppermute(values, axis, [(i, i ^ by) for i in range(size)])  13 us
    pallas_call x1, Pallas kernels, hidden_slice(): pl.pallas_call(slice_kernel, grid_spec=pltpu.PrefetchScalarGridSpec(num_s...  11.5 us
    pallas_call x1, Pallas kernels, forward(): pl.pallas_call(forward_kernel, in_specs=[VM, VM, IN_HBM, IN_HBM], out_spe...  9.17 us
    pallas_call x1, Pallas kernels, backward(): pl.pallas_call(backward_kernel, in_specs=[pl.BlockSpec(memory_space=pltpu...  7.58 us
    unnamed x32, local copies, waits for them, and re-layouts  4.98 us
  transfers between devices with their start and end apart: 10, of which 3 were waited for; matrix products, arithmetic and copies ran while one was open for 0% of the time, Pallas kernels for 32%

profile of v2, /device:TPU:1, one launch (start us, length us, event | category | flops | bytes accessed | tf_op | source)
XLA Modules:
  0.0 139.9 jit_solution(17041621346382178028)
XLA Ops:
  7.2 0.0 all-gather.4.cloned.1.call-start
  7.2 2.2 %shard_map.130 = (bf16[1792,128]{1,0:T(8,128)(2,1)}, f32[132,1]{1,0:T(8,128)}, f32[2,768]{1,0:T(2,128)}) custom-call(bf16[132,768]{1,0:T(8,128)(2,1)} %x.1, s32[1,132]{1,0:T(1,128)} %bitcast.33, s32[1,132]{1,0:T(1,128)} %bitcast.34, f32[1,132]{1,0:T(1,128)} %bitcast.35, f32[768]{0:T(1024)} %gain_in.1, f32[768]{0:T(1024)} %gain_out.1), custom_call_target="tpu_custom_call" | custom-call | flops 58392576 | bytes 700000 | tf_op jit(solution)/shard_map/pallas_call | solution.py:159
  9.4 24.9 %all_to_all.20 = bf16[32,56,128]{2,1,0:T(8,128)(2,1)} all-to-all(bf16[32,56,128]{2,1,0:T(8,128)(2,1)} %bitcast.32), channel_id=1, replica_groups=mesh['expert'=32,'dp'=8] {'expert'}, dimensions={0} | all-to-all | bytes 917504 | tf_op jit(solution)/shard_map/all_to_all | solution.py:564
  34.3 0.0 all-gather.4.cloned.1.call-update
  34.3 0.0 all-gather.6.cloned.1.call-start
  34.4 1.0 copy-done.3
  35.4 0.7 copy-done.6
  36.1 9.2 %shard_map.131 = (bf16[128,768]{1,0:T(8,128)(2,1)S(1)}, bf16[304,768]{1,0:T(8,128)(2,1)}, bf16[288,3072]{1,0:T(8,128)(2,1)S(1)}, bf16[288,256]{1,0:T(8,128)(2,1)S(1)}, bf16[288,768]{1,0:T(8,128)(2,1)S(1)}) custom-call(bf16[1792,128]{1,0:T(8,128)(2,1)S(1)} %bitcast.25, f32[2,768]{1,0:T(2,128)S(1)} %copy-done.6, bf16[768,3072]{1,0:T(8,128)(2,1)} %bitcast.16, ...), custom_call_target="tpu_custom_call" | custom-call | flops 2717908992 | bytes 9437184 | tf_op jit(solution)/shard_map/pallas_call | solution.py:236
  45.3 0.0 all-gather.6.cloned.1.call-update
  45.3 14.2 %all_to_all.21 = bf16[8,16,768]{2,1,0:T(8,128)(2,1)S(1)} all-to-all(bf16[8,16,768]{2,1,0:T(8,128)(2,1)S(1)} %bitcast.31), channel_id=1, replica_groups={{0,8,16,24,32,40,48,56},{64,72,80,88,96,104,112,120},{128,136,144,152,1..., dimensions={0} | all-to-all | bytes 393216 | tf_op jit(solution)/shard_map/all_to_all | solution.py:569
  59.6 1.7 %collective-permute-start.1 = (f32[16,768]{1,0:T(8,128)S(1)}, f32[16,768]{1,0:T(8,128)S(1)}, u32[]{:S(2)}, u32[]{:S(2)}) collective-permute-start(f32[16,768]{1,0:T(8,128)S(1)} %convert_reduce_fusion), channel_id=1, source_target_pairs={{0,128},{8,136},{16,144},{24,152},{32,160},{40,168},{48,176},{56,1... | collective-permute-start | bytes 147464 | tf_op jit(solution)/shard_map/ppermute | solution.py:575
  61.3 1.5 %collective-permute-start.2 = (f32[16,768]{1,0:T(8,128)S(1)}, f32[16,768]{1,0:T(8,128)S(1)}, u32[]{:S(2)}, u32[]{:S(2)}) collective-permute-start(f32[16,768]{1,0:T(8,128)S(1)} %convert_reduce_fusion), channel_id=1, source_target_pairs={{0,192},{8,200},{16,208},{24,216},{32,224},{40,232},{48,240},{56,2... | collective-permute-start | bytes 147464 | tf_op jit(solution)/shard_map/ppermute | solution.py:575
  62.8 0.0 collective-permute-start
  62.8 1.4 collective-permute-done.1
  64.2 1.7 %collective-permute-done.2 = f32[16,768]{1,0:T(8,128)S(1)} collective-permute-done((f32[16,768]{1,0:T(8,128)S(1)}, f32[16,768]{1,0:T(8,128)S(1)}, u32[]{:S(2)}, u32[]{:S(2)}) %collective-permute-start.2) | collective-permute-done | bytes 49184 | tf_op jit(solution)/shard_map/ppermute | solution.py:575
  65.8 0.1 collective-permute-done
  65.9 0.1 multiply_convert_fusion
  66.0 11.2 %all_to_all.22 = bf16[8,16,768]{2,1,0:T(8,128)(2,1)S(1)} all-to-all(bf16[8,16,768]{2,1,0:T(8,128)(2,1)S(1)} %broadcast_in_dim.23), channel_id=1, replica_groups={{0,8,16,24,32,40,48,56},{64,72,80,88,96,104,112,120},{128,136,144,152,1..., dimensions={0} | all-to-all | bytes 393216 | tf_op jit(solution)/shard_map/all_to_all | solution.py:569
  77.3 0.9 collective-permute-start.3
  78.2 3.0 %collective-permute-start.4 = (bf16[128,768]{1,0:T(8,128)(2,1)S(1)}, bf16[128,768]{1,0:T(8,128)(2,1)S(1)}, u32[]{:S(2)}, u32[]{:S(2)}) collective-permute-start(bf16[128,768]{1,0:T(8,128)(2,1)S(1)} %bitcast.28), channel_id=1, source_target_pairs={{0,4},{1,5},{2,6},{3,7},{4,0},{5,1},{6,2},{7,3},{8,12},{9,13},{10,... | collective-permute-start | bytes 589832 | tf_op jit(solution)/shard_map/ppermute | solution.py:575
  81.2 0.0 collective-permute-start.5
  81.2 0.0 copy-done.7
  81.2 0.0 copy-start.1
  81.2 2.6 %copy-done.1 = bf16[8,1792,128]{2,1,0:T(8,128)(2,1)S(1)} copy-done((bf16[8,1792,128]{2,1,0:T(8,128)(2,1)S(1)}, bf16[8,1792,128]{2,1,0:T(8,128)(2,1)}, u32[]{:S(2)}) %copy-start.1) | copy-done | bytes 3670040
  83.8 11.5 %shard_map.132 = (bf16[768,2304]{1,0:T(8,128)(2,1)S(1)}, bf16[384,2304]{1,0:T(8,128)(2,1)S(1)}, bf16[2304,384]{1,0:T(8,128)(2,1)S(1)}, bf16[128,768]{1,0:T(8,128)(2,1)S(1)}) custom-call(s32[1]{0:T(128)} %bitcast.dp, bf16[8,1792,128]{2,1,0:T(8,128)(2,1)S(1)} %copy-done.1, f32[2,768]{1,0:T(2,128)S(1)} %copy-done.7, bf16[768,3072]{1,0:T(8,128)(2,1)} %bitcast.17, ...), custom_call_target="tpu_custom_call" | custom-call | flops 1358954496 | bytes 12000000 | tf_op jit(solution)/shard_map/pallas_call | solution.py:419
  95.4 0.0 collective-permute-done.3.b
  95.4 0.0 collective-permute-done.4.c
  95.4 0.0 collective-permute-done.5.d
  95.4 0.1 shard_map.133.near
  95.5 5.9 %collective-permute-start.6 = (bf16[512,768]{1,0:T(8,128)(2,1)S(1)}, bf16[512,768]{1,0:T(8,128)(2,1)S(1)}, u32[]{:S(2)}, u32[]{:S(2)}) collective-permute-start(bf16[512,768]{1,0:T(8,128)(2,1)S(1)} %shard_map.133.near), channel_id=1, source_target_pairs={{0,1},{1,0},{2,3},{3,2},{4,5},{5,4},{6,7},{7,6},{8,9},{9,8},{10,11... | collective-permute-start | bytes 2359304 | tf_op jit(solution)/shard_map/ppermute | solution.py:575
  103.3 0.1 pad_maximum_fusion.scalars
  103.3 0.0 collective-permute-done.6.far
  103.4 0.0 slice-done
  103.4 0.0 slice-done.1
  103.4 0.0 copy-done
  103.4 7.6 %shard_map.134 = (bf16[1792,128]{1,0:T(8,128)(2,1)}, f32[8,128]{1,0:T(8,128)S(1)}) custom-call(f32[3]{0:T(128)S(1)} %pad_maximum_fusion.scalars, bf16[512,768]{1,0:T(8,128)(2,1)S(1)} %shard_map.133.near, bf16[512,768]{1,0:T(8,128)(2,1)S(1)} %collective-permute-done.6.far, f32[2,768]{1,0:T(2,128)S(1)} %copy-done.7, ...), custom_call_target="tpu_custom_call" | custom-call | flops 3019898880 | bytes 11206656 | tf_op jit(solution)/shard_map/pallas_call | solution.py:362
  111.0 0.0 copy-done.2
  111.0 0.0 copy-done.9
  111.0 0.0 copy-done.4
  111.0 0.0 copy-start.13
  111.0 4.1 %all-to-all-start.3 = ((bf16[32,56,128]{2,1,0:T(8,128)(2,1)}), bf16[32,56,128]{2,1,0:T(8,128)(2,1)S(1)}, u32[]{:S(2)}, u32[]{:S(2)}) async-start(bf16[32,56,128]{2,1,0:T(8,128)(2,1)} %bitcast.11), calls=%async_computation.3 | async-start | bytes 917504 | tf_op jit(solution)/shard_map/all_to_all | solution.py:564
  115.1 0.0 all-gather.6.cloned.1.call-done
  115.2 0.0 copy-start.5
  115.2 16.1 %shard_map.135 = (bf16[768,384]{1,0:T(8,128)(2,1)}, bf16[384,768]{1,0:T(8,128)(2,1)}, f32[8,128]{1,0:T(8,128)}) custom-call(s32[1]{0:T(128)} %bitcast.dp, f32[3]{0:T(128)} %copy-done.9, bf16[512,768]{1,0:T(8,128)(2,1)} %copy-done.2, bf16[512,768]{1,0:T(8,128)(2,1)} %copy-done.4, f32[2,768]{1,0:T(2,128)} %get-tuple-element.21.gains, ...), custom_call_target="tpu_custom_call" | custom-call | flops 6090129408 | bytes 15000000 | tf_op jit(solution)/shard_map/pallas_call | solution.py:500
  131.3 0.0 all-to-all-done.3
  131.3 0.0 copy-done.5
  131.3 0.7 copy-done.8
  132.0 1.1 shard_map.136
  (22 shorter events, 0.1 us)
Async XLA Ops:
  7.2 74.0 %all-gather.4.cloned.1.call-start = ((), (), s32[]{:S(2)}) async-start(), calls=%async_computation.4 | async-start | bytes 4128768 | tf_op jit(solution)/shard_map/all_gather | solution.py:604
  34.3 80.8 %all-gather.6.cloned.1.call-start = ((), (), s32[]{:S(2)}) async-start(), calls=%async_computation.5 | async-start | bytes 4202496 | tf_op jit(solution)/shard_map/all_gather | solution.py:606
  34.4 1.0 copy-start.3
  35.4 0.7 copy-start.6
  36.1 45.1 %copy-start.7 = (f32[2,768]{1,0:T(2,128)S(1)}, f32[2,768]{1,0:T(2,128)}, u32[]{:S(2)}) copy-start(f32[2,768]{1,0:T(2,128)} %get-tuple-element.21.gains) | copy-start | bytes 18436
  59.6 4.6 %collective-permute-start.1 = (f32[16,768]{1,0:T(8,128)S(1)}, f32[16,768]{1,0:T(8,128)S(1)}, u32[]{:S(2)}, u32[]{:S(2)}) collective-permute-start(f32[16,768]{1,0:T(8,128)S(1)} %convert_reduce_fusion), channel_id=1, source_target_pairs={{0,128},{8,136},{16,144},{24,152},{32,160},{40,168},{48,176},{56,1... | collective-permute-start | bytes 147464 | tf_op jit(solution)/shard_map/ppermute | solution.py:575
  61.3 4.6 %collective-permute-start.2 = (f32[16,768]{1,0:T(8,128)S(1)}, f32[16,768]{1,0:T(8,128)S(1)}, u32[]{:S(2)}, u32[]{:S(2)}) collective-permute-start(f32[16,768]{1,0:T(8,128)S(1)} %convert_reduce_fusion), channel_id=1, source_target_pairs={{0,192},{8,200},{16,208},{24,216},{32,224},{40,232},{48,240},{56,2... | collective-permute-start | bytes 147464 | tf_op jit(solution)/shard_map/ppermute | solution.py:575
  62.8 3.2 %collective-permute-start = (f32[16,768]{1,0:T(8,128)S(1)}, f32[16,768]{1,0:T(8,128)S(1)}, u32[]{:S(2)}, u32[]{:S(2)}) collective-permute-start(f32[16,768]{1,0:T(8,128)S(1)} %convert_reduce_fusion), channel_id=1, source_target_pairs={{0,64},{8,72},{16,80},{24,88},{32,96},{40,104},{48,112},{56,120},{... | collective-permute-start | bytes 147464 | tf_op jit(solution)/shard_map/ppermute | solution.py:575
  77.3 18.1 %collective-permute-start.3 = (bf16[128,768]{1,0:T(8,128)(2,1)S(1)}, bf16[128,768]{1,0:T(8,128)(2,1)S(1)}, u32[]{:S(2)}, u32[]{:S(2)}) collective-permute-start(bf16[128,768]{1,0:T(8,128)(2,1)S(1)} %bitcast.27), channel_id=1, source_target_pairs={{0,2},{1,3},{2,0},{3,1},{4,6},{5,7},{6,4},{7,5},{8,10},{9,11},{10,... | collective-permute-start | bytes 589832 | tf_op jit(solution)/shard_map/ppermute | solution.py:575
  78.2 17.2 %collective-permute-start.4 = (bf16[128,768]{1,0:T(8,128)(2,1)S(1)}, bf16[128,768]{1,0:T(8,128)(2,1)S(1)}, u32[]{:S(2)}, u32[]{:S(2)}) collective-permute-start(bf16[128,768]{1,0:T(8,128)(2,1)S(1)} %bitcast.28), channel_id=1, source_target_pairs={{0,4},{1,5},{2,6},{3,7},{4,0},{5,1},{6,2},{7,3},{8,12},{9,13},{10,... | collective-permute-start | bytes 589832 | tf_op jit(solution)/shard_map/ppermute | solution.py:575
  81.2 14.2 %collective-permute-start.5 = (bf16[128,768]{1,0:T(8,128)(2,1)S(1)}, bf16[128,768]{1,0:T(8,128)(2,1)S(1)}, u32[]{:S(2)}, u32[]{:S(2)}) collective-permute-start(bf16[128,768]{1,0:T(8,128)(2,1)S(1)} %bitcast.29), channel_id=1, source_target_pairs={{0,6},{1,7},{2,4},{3,5},{4,2},{5,3},{6,0},{7,1},{8,14},{9,15},{10,... | collective-permute-start | bytes 589832 | tf_op jit(solution)/shard_map/ppermute | solution.py:575
  81.2 22.2 %slice-start = ((s8[4718592]{0:T(1024)(128)(4,1)}), s8[4194304]{0:T(1024)(128)(4,1)S(1)}, s32[]{:S(2)}) async-start(s8[4718592]{0:T(1024)(128)(4,1)} %bitcast.18), calls=%async_computation.6 | async-start | bytes 8388608
  81.2 2.6 %copy-start.1 = (bf16[8,1792,128]{2,1,0:T(8,128)(2,1)S(1)}, bf16[8,1792,128]{2,1,0:T(8,128)(2,1)}, u32[]{:S(2)}) copy-start(bf16[8,1792,128]{2,1,0:T(8,128)(2,1)} %all-gather.4.cloned.1.call-done.arr) | copy-start | bytes 11010052
  83.8 19.6 %slice-start.1 = ((s8[4718592]{0:T(1024)(128)(4,1)}), s8[524288]{0:T(1024)(128)(4,1)S(1)}, s32[]{:S(2)}) async-start(s8[4718592]{0:T(1024)(128)(4,1)} %bitcast.18), calls=%async_computation.7 | async-start | bytes 1048576
  83.8 19.6 %copy-start = (bf16[1,3072,768]{2,1,0:T(8,128)(2,1)S(1)}, bf16[1,3072,768]{2,1,0:T(8,128)(2,1)}, u32[]{:S(2)}) copy-start(bf16[1,3072,768]{2,1,0:T(8,128)(2,1)} %param.18) | copy-start | bytes 14155780
  95.3 15.6 %copy-start.10 = (bf16[768,2304]{1,0:T(8,128)(2,1)}, bf16[768,2304]{1,0:T(8,128)(2,1)S(1)}, u32[]{:S(2)}) copy-start(bf16[768,2304]{1,0:T(8,128)(2,1)S(1)} %get-tuple-element.32.normed_t) | copy-start | bytes 10616836
  95.3 15.6 %copy-start.11 = (bf16[384,2304]{1,0:T(8,128)(2,1)}, bf16[384,2304]{1,0:T(8,128)(2,1)S(1)}, u32[]{:S(2)}) copy-start(bf16[384,2304]{1,0:T(8,128)(2,1)S(1)} %get-tuple-element.33.hidden_t) | copy-start | bytes 5308420
  95.4 15.6 %copy-start.12 = (bf16[2304,384]{1,0:T(8,128)(2,1)}, bf16[2304,384]{1,0:T(8,128)(2,1)S(1)}, u32[]{:S(2)}) copy-start(bf16[2304,384]{1,0:T(8,128)(2,1)S(1)} %get-tuple-element.30.slope) | copy-start | bytes 5308420
  95.5 15.5 %copy-start.2 = (bf16[512,768]{1,0:T(8,128)(2,1)}, bf16[512,768]{1,0:T(8,128)(2,1)S(1)}, u32[]{:S(2)}) copy-start(bf16[512,768]{1,0:T(8,128)(2,1)S(1)} %shard_map.133.near) | copy-start | bytes 2359300
  95.5 7.9 %collective-permute-start.6 = (bf16[512,768]{1,0:T(8,128)(2,1)S(1)}, bf16[512,768]{1,0:T(8,128)(2,1)S(1)}, u32[]{:S(2)}, u32[]{:S(2)}) collective-permute-start(bf16[512,768]{1,0:T(8,128)(2,1)S(1)} %shard_map.133.near), channel_id=1, source_target_pairs={{0,1},{1,0},{2,3},{3,2},{4,5},{5,4},{6,7},{7,6},{8,9},{9,8},{10,11... | collective-permute-start | bytes 2359304 | tf_op jit(solution)/shard_map/ppermute | solution.py:575
  103.3 7.6 %copy-start.9 = (f32[3]{0:T(128)}, f32[3]{0:T(128)S(1)}, u32[]{:S(2)}) copy-start(f32[3]{0:T(128)S(1)} %pad_maximum_fusion.scalars) | copy-start | bytes 40
  103.4 7.7 %copy-start.4 = (bf16[512,768]{1,0:T(8,128)(2,1)}, bf16[512,768]{1,0:T(8,128)(2,1)S(1)}, u32[]{:S(2)}) copy-start(bf16[512,768]{1,0:T(8,128)(2,1)S(1)} %collective-permute-done.6.far) | copy-start | bytes 2359300
  111.0 4.2 %copy-start.13 = (f32[8,128]{1,0:T(8,128)}, f32[8,128]{1,0:T(8,128)S(1)}, u32[]{:S(2)}) copy-start(f32[8,128]{1,0:T(8,128)S(1)} %get-tuple-element.31._) | copy-start | bytes 12292
  111.0 20.2 %all-to-all-start.3 = ((bf16[32,56,128]{2,1,0:T(8,128)(2,1)}), bf16[32,56,128]{2,1,0:T(8,128)(2,1)S(1)}, u32[]{:S(2)}, u32[]{:S(2)}) async-start(bf16[32,56,128]{2,1,0:T(8,128)(2,1)} %bitcast.11), calls=%async_computation.3 | async-start | bytes 917504 | tf_op jit(solution)/shard_map/all_to_all | solution.py:564
  115.2 16.1 %copy-start.5 = (f32[132,1]{1,0:T(8,128)S(1)}, f32[132,1]{1,0:T(8,128)}, u32[]{:S(2)}) copy-start(f32[132,1]{1,0:T(8,128)} %get-tuple-element.29.slot) | copy-start | bytes 1588
  131.3 0.7 copy-start.8
Sparse Core Ops, SparseCore 0:
  34.5 33.0 all-gather.3
  69.9 39.7 all-gather.5

commit v3 on v2

--- a/solution.py
+++ b/solution.py
@@ -295,9 +295,8 @@
     load_units(near, far, unit, inverse, img, txt, 1)
 
     def side(mine, others):
-        hi, low = two(slopes(scalars, dot(mine[:HALF, :], others[...], 1, 1)))
-        both = dot(jnp.concatenate([hi, low], axis=0), others[...])
-        return both[:HALF] + both[HALF:]
+        slope = slopes(scalars, dot(mine[:HALF, :], others[...], 1, 1))
+        return dot(slope.astype(BF), others[...])
 
     return pool_grads(side(img, txt), side(txt, img), unit[...], inverse[...], gains[1:2, :])
 
@@ -606,9 +605,10 @@
     bundles = lax.all_gather(bundle, "dp", axis=0)
 
     part = along_z(part.reshape(NZ, 2 * NZ, D))
-    part = jnp.sum(part.astype(F32), axis=0)
+    part = jnp.sum(part.astype(F32), axis=0).astype(BF)
     others = [swap(part, "expert", E, NZ * m) for m in range(1, NX)]
     share = jnp.where(jnp.arange(2 * NZ) < NZ, 1.0 / IMG, 1.0 / TXT).astype(F32)
+    part, others = part.astype(F32), [other.astype(F32) for other in others]
     pooled = (((part + others[0]) + (others[1] + others[2])) * share[:, None]).astype(BF)
     pooled = along_z(jnp.broadcast_to(pooled[None], (NZ, 2 * NZ, D))).reshape(GROUP, D)
     normed_t, hidden_t, grads, passed = hidden_slice(dp, arrs, gains, w1, pooled)

time: 140 us -> 140 us (level)
  no operation moved by 1% of the time
where the time goes in v3:
time: 140 us; the launch traced here: 139 us
  blocking collectives  50.2 us (36%)
  Pallas kernels  48 us (34%)
  starting transfers between devices  17.3 us (12%)
  between operations  16.2 us (12%)
  local copies, waits for them, and re-layouts  4.85 us (3%)
  waiting for transfers between devices  2.4 us (2%)
    all_to_all x2, blocking collectives, along_z(): lax.all_to_all(values, 'expert', split_axis=0, concat_axis=0, tiled=True,...  25.3 us
    all_to_all x1, blocking collectives, to_experts(): lax.all_to_all(slabs, 'expert', split_axis=0, concat_axis=0, tiled=True)  24.9 us
    pallas_call x1, Pallas kernels, weight_grads(): pl.pallas_call(weights_kernel, grid_spec=pltpu.PrefetchScalarGridSpec(num...  16.1 us
    ppermute x7, starting transfers between devices, swap(): return lax.ppermute(values, axis, [(i, i ^ by) for i in range(size)])  13 us
    pallas_call x1, Pallas kernels, hidden_slice(): pl.pallas_call(slice_kernel, grid_spec=pltpu.PrefetchScalarGridSpec(num_s...  11.9 us
    pallas_call x1, Pallas kernels, forward(): pl.pallas_call(forward_kernel, in_specs=[VM, VM, IN_HBM, IN_HBM], out_spe...  9.17 us
    pallas_call x1, Pallas kernels, backward(): pl.pallas_call(backward_kernel, in_specs=[pl.BlockSpec(memory_space=pltpu...  7.54 us
    unnamed x32, local copies, waits for them, and re-layouts  4.83 us
  transfers between devices with their start and end apart: 10, of which 3 were waited for; matrix products, arithmetic and copies ran while one was open for 0% of the time, Pallas kernels for 32%

profile of v3, /device:TPU:1, one launch (start us, length us, event | category | flops | bytes accessed | tf_op | source)
XLA Modules:
  0.0 139.1 jit_solution(2357091617696443209)
XLA Ops:
  7.2 0.0 all-gather.4.cloned.1.call-start
  7.2 2.2 %shard_map.130 = (bf16[1792,128]{1,0:T(8,128)(2,1)}, f32[132,1]{1,0:T(8,128)}, f32[2,768]{1,0:T(2,128)}) custom-call(bf16[132,768]{1,0:T(8,128)(2,1)} %x.1, s32[1,132]{1,0:T(1,128)} %bitcast.33, s32[1,132]{1,0:T(1,128)} %bitcast.34, f32[1,132]{1,0:T(1,128)} %bitcast.35, f32[768]{0:T(1024)} %gain_in.1, f32[768]{0:T(1024)} %gain_out.1), custom_call_target="tpu_custom_call" | custom-call | flops 58392576 | bytes 700000 | tf_op jit(solution)/shard_map/pallas_call | solution.py:159
  9.4 24.9 %all_to_all.20 = bf16[32,56,128]{2,1,0:T(8,128)(2,1)} all-to-all(bf16[32,56,128]{2,1,0:T(8,128)(2,1)} %bitcast.32), channel_id=1, replica_groups=mesh['expert'=32,'dp'=8] {'expert'}, dimensions={0} | all-to-all | bytes 917504 | tf_op jit(solution)/shard_map/all_to_all | solution.py:563
  34.3 0.0 all-gather.4.cloned.1.call-update
  34.3 0.0 all-gather.6.cloned.1.call-start
  34.4 0.0 copy-start.3
  34.4 1.0 copy-done.3
  35.4 0.7 copy-done.6
  36.1 9.2 %shard_map.131 = (bf16[128,768]{1,0:T(8,128)(2,1)S(1)}, bf16[304,768]{1,0:T(8,128)(2,1)}, bf16[288,3072]{1,0:T(8,128)(2,1)S(1)}, bf16[288,256]{1,0:T(8,128)(2,1)S(1)}, bf16[288,768]{1,0:T(8,128)(2,1)S(1)}) custom-call(bf16[1792,128]{1,0:T(8,128)(2,1)S(1)} %bitcast.25, f32[2,768]{1,0:T(2,128)S(1)} %copy-done.6, bf16[768,3072]{1,0:T(8,128)(2,1)} %bitcast.16, ...), custom_call_target="tpu_custom_call" | custom-call | flops 2717908992 | bytes 9437184 | tf_op jit(solution)/shard_map/pallas_call | solution.py:236
  45.3 0.0 all-gather.6.cloned.1.call-update
  45.3 14.2 %all_to_all.21 = bf16[8,16,768]{2,1,0:T(8,128)(2,1)S(1)} all-to-all(bf16[8,16,768]{2,1,0:T(8,128)(2,1)S(1)} %bitcast.31), channel_id=1, replica_groups={{0,8,16,24,32,40,48,56},{64,72,80,88,96,104,112,120},{128,136,144,152,1..., dimensions={0} | all-to-all | bytes 393216 | tf_op jit(solution)/shard_map/all_to_all | solution.py:568
  59.6 1.3 collective-permute-start.2
  60.9 1.3 collective-permute-start.1
  62.2 0.7 collective-permute-start
  62.9 1.0 collective-permute-done.2
  64.0 1.2 collective-permute-done.1
  65.1 0.1 collective-permute-done
  65.3 0.1 multiply_convert_fusion
  65.4 11.0 %all_to_all.22 = bf16[8,16,768]{2,1,0:T(8,128)(2,1)S(1)} all-to-all(bf16[8,16,768]{2,1,0:T(8,128)(2,1)S(1)} %broadcast_in_dim.23), channel_id=1, replica_groups={{0,8,16,24,32,40,48,56},{64,72,80,88,96,104,112,120},{128,136,144,152,1..., dimensions={0} | all-to-all | bytes 393216 | tf_op jit(solution)/shard_map/all_to_all | solution.py:568
  76.4 1.1 collective-permute-start.3
  77.5 2.6 %collective-permute-start.4 = (bf16[128,768]{1,0:T(8,128)(2,1)S(1)}, bf16[128,768]{1,0:T(8,128)(2,1)S(1)}, u32[]{:S(2)}, u32[]{:S(2)}) collective-permute-start(bf16[128,768]{1,0:T(8,128)(2,1)S(1)} %bitcast.28), channel_id=1, source_target_pairs={{0,4},{1,5},{2,6},{3,7},{4,0},{5,1},{6,2},{7,3},{8,12},{9,13},{10,... | collective-permute-start | bytes 589832 | tf_op jit(solution)/shard_map/ppermute | solution.py:574
  80.1 0.1 collective-permute-start.5
  80.3 0.0 copy-done.7
  80.3 2.4 %copy-done.1 = bf16[8,1792,128]{2,1,0:T(8,128)(2,1)S(1)} copy-done((bf16[8,1792,128]{2,1,0:T(8,128)(2,1)S(1)}, bf16[8,1792,128]{2,1,0:T(8,128)(2,1)}, u32[]{:S(2)}) %copy-start.1) | copy-done | bytes 3670040
  82.7 11.9 %shard_map.132 = (bf16[768,2304]{1,0:T(8,128)(2,1)S(1)}, bf16[384,2304]{1,0:T(8,128)(2,1)S(1)}, bf16[2304,384]{1,0:T(8,128)(2,1)S(1)}, bf16[128,768]{1,0:T(8,128)(2,1)S(1)}) custom-call(s32[1]{0:T(128)} %bitcast.dp, bf16[8,1792,128]{2,1,0:T(8,128)(2,1)S(1)} %copy-done.1, f32[2,768]{1,0:T(2,128)S(1)} %copy-done.7, bf16[768,3072]{1,0:T(8,128)(2,1)} %bitcast.17, ...), custom_call_target="tpu_custom_call" | custom-call | flops 1358954496 | bytes 12000000 | tf_op jit(solution)/shard_map/pallas_call | solution.py:418
  94.5 0.0 copy-start.10
  94.6 0.0 copy-start.11
  94.6 0.0 copy-start.12
  94.6 0.0 collective-permute-done.3.b
  94.6 0.0 collective-permute-done.4.c
  94.6 0.0 collective-permute-done.5.d
  94.6 0.1 shard_map.133.near
  94.7 0.0 copy-start.2
  94.7 5.8 %collective-permute-start.6 = (bf16[512,768]{1,0:T(8,128)(2,1)S(1)}, bf16[512,768]{1,0:T(8,128)(2,1)S(1)}, u32[]{:S(2)}, u32[]{:S(2)}) collective-permute-start(bf16[512,768]{1,0:T(8,128)(2,1)S(1)} %shard_map.133.near), channel_id=1, source_target_pairs={{0,1},{1,0},{2,3},{3,2},{4,5},{5,4},{6,7},{7,6},{8,9},{9,8},{10,11... | collective-permute-start | bytes 2359304 | tf_op jit(solution)/shard_map/ppermute | solution.py:574
  102.4 0.1 pad_maximum_fusion.scalars
  102.5 0.0 collective-permute-done.6.far
  102.5 0.0 slice-done
  102.5 0.0 slice-done.1
  102.5 7.5 %shard_map.134 = (bf16[1792,128]{1,0:T(8,128)(2,1)}, f32[8,128]{1,0:T(8,128)S(1)}) custom-call(f32[3]{0:T(128)S(1)} %pad_maximum_fusion.scalars, bf16[512,768]{1,0:T(8,128)(2,1)S(1)} %shard_map.133.near, bf16[512,768]{1,0:T(8,128)(2,1)S(1)} %collective-permute-done.6.far, f32[2,768]{1,0:T(2,128)S(1)} %copy-done.7, ...), custom_call_target="tpu_custom_call" | custom-call | flops 3019898880 | bytes 11206656 | tf_op jit(solution)/shard_map/pallas_call | solution.py:361
  110.1 0.0 copy-done.11
  110.1 4.2 %all-to-all-start.3 = ((bf16[32,56,128]{2,1,0:T(8,128)(2,1)}), bf16[32,56,128]{2,1,0:T(8,128)(2,1)S(1)}, u32[]{:S(2)}, u32[]{:S(2)}) async-start(bf16[32,56,128]{2,1,0:T(8,128)(2,1)} %bitcast.11), calls=%async_computation.3 | async-start | bytes 917504 | tf_op jit(solution)/shard_map/all_to_all | solution.py:563
  114.3 0.0 all-gather.6.cloned.1.call-done
  114.4 0.0 copy-done.13
  114.4 0.0 copy-start.5
  114.4 16.1 %shard_map.135 = (bf16[768,384]{1,0:T(8,128)(2,1)}, bf16[384,768]{1,0:T(8,128)(2,1)}, f32[8,128]{1,0:T(8,128)}) custom-call(s32[1]{0:T(128)} %bitcast.dp, f32[3]{0:T(128)} %copy-done.9, bf16[512,768]{1,0:T(8,128)(2,1)} %copy-done.2, bf16[512,768]{1,0:T(8,128)(2,1)} %copy-done.4, f32[2,768]{1,0:T(2,128)} %get-tuple-element.21.gains, ...), custom_call_target="tpu_custom_call" | custom-call | flops 6090129408 | bytes 15000000 | tf_op jit(solution)/shard_map/pallas_call | solution.py:499
  130.5 0.0 all-to-all-done.3
  130.5 0.7 copy-done.8
  131.2 1.1 shard_map.136
  (22 shorter events, 0.1 us)
Async XLA Ops:
  7.2 73.1 %all-gather.4.cloned.1.call-start = ((), (), s32[]{:S(2)}) async-start(), calls=%async_computation.4 | async-start | bytes 4128768 | tf_op jit(solution)/shard_map/all_gather | solution.py:603
  34.3 80.0 %all-gather.6.cloned.1.call-start = ((), (), s32[]{:S(2)}) async-start(), calls=%async_computation.5 | async-start | bytes 4202496 | tf_op jit(solution)/shard_map/all_gather | solution.py:605
  34.4 1.0 copy-start.3
  35.4 0.7 copy-start.6
  36.1 44.2 %copy-start.7 = (f32[2,768]{1,0:T(2,128)S(1)}, f32[2,768]{1,0:T(2,128)}, u32[]{:S(2)}) copy-start(f32[2,768]{1,0:T(2,128)} %get-tuple-element.21.gains) | copy-start | bytes 18436
  59.6 4.4 %collective-permute-start.2 = (bf16[16,768]{1,0:T(8,128)(2,1)S(1)}, bf16[16,768]{1,0:T(8,128)(2,1)S(1)}, u32[]{:S(2)}, u32[]{:S(2)}) collective-permute-start(bf16[16,768]{1,0:T(8,128)(2,1)S(1)} %reduce_sum.12), channel_id=1, source_target_pairs={{0,192},{8,200},{16,208},{24,216},{32,224},{40,232},{48,240},{56,2... | collective-permute-start | bytes 73736 | tf_op jit(solution)/shard_map/ppermute | solution.py:574
  60.9 4.2 %collective-permute-start.1 = (bf16[16,768]{1,0:T(8,128)(2,1)S(1)}, bf16[16,768]{1,0:T(8,128)(2,1)S(1)}, u32[]{:S(2)}, u32[]{:S(2)}) collective-permute-start(bf16[16,768]{1,0:T(8,128)(2,1)S(1)} %reduce_sum.12), channel_id=1, source_target_pairs={{0,128},{8,136},{16,144},{24,152},{32,160},{40,168},{48,176},{56,1... | collective-permute-start | bytes 73736 | tf_op jit(solution)/shard_map/ppermute | solution.py:574
  62.2 3.1 %collective-permute-start = (bf16[16,768]{1,0:T(8,128)(2,1)S(1)}, bf16[16,768]{1,0:T(8,128)(2,1)S(1)}, u32[]{:S(2)}, u32[]{:S(2)}) collective-permute-start(bf16[16,768]{1,0:T(8,128)(2,1)S(1)} %reduce_sum.12), channel_id=1, source_target_pairs={{0,64},{8,72},{16,80},{24,88},{32,96},{40,104},{48,112},{56,120},{... | collective-permute-start | bytes 73736 | tf_op jit(solution)/shard_map/ppermute | solution.py:574
  76.4 18.2 %collective-permute-start.3 = (bf16[128,768]{1,0:T(8,128)(2,1)S(1)}, bf16[128,768]{1,0:T(8,128)(2,1)S(1)}, u32[]{:S(2)}, u32[]{:S(2)}) collective-permute-start(bf16[128,768]{1,0:T(8,128)(2,1)S(1)} %bitcast.27), channel_id=1, source_target_pairs={{0,2},{1,3},{2,0},{3,1},{4,6},{5,7},{6,4},{7,5},{8,10},{9,11},{10,... | collective-permute-start | bytes 589832 | tf_op jit(solution)/shard_map/ppermute | solution.py:574
  77.5 17.1 %collective-permute-start.4 = (bf16[128,768]{1,0:T(8,128)(2,1)S(1)}, bf16[128,768]{1,0:T(8,128)(2,1)S(1)}, u32[]{:S(2)}, u32[]{:S(2)}) collective-permute-start(bf16[128,768]{1,0:T(8,128)(2,1)S(1)} %bitcast.28), channel_id=1, source_target_pairs={{0,4},{1,5},{2,6},{3,7},{4,0},{5,1},{6,2},{7,3},{8,12},{9,13},{10,... | collective-permute-start | bytes 589832 | tf_op jit(solution)/shard_map/ppermute | solution.py:574
  80.1 14.5 %collective-permute-start.5 = (bf16[128,768]{1,0:T(8,128)(2,1)S(1)}, bf16[128,768]{1,0:T(8,128)(2,1)S(1)}, u32[]{:S(2)}, u32[]{:S(2)}) collective-permute-start(bf16[128,768]{1,0:T(8,128)(2,1)S(1)} %bitcast.29), channel_id=1, source_target_pairs={{0,6},{1,7},{2,4},{3,5},{4,2},{5,3},{6,0},{7,1},{8,14},{9,15},{10,... | collective-permute-start | bytes 589832 | tf_op jit(solution)/shard_map/ppermute | solution.py:574
  80.3 22.2 %slice-start = ((s8[4718592]{0:T(1024)(128)(4,1)}), s8[4194304]{0:T(1024)(128)(4,1)S(1)}, s32[]{:S(2)}) async-start(s8[4718592]{0:T(1024)(128)(4,1)} %bitcast.18), calls=%async_computation.6 | async-start | bytes 8388608
  80.3 2.4 %copy-start.1 = (bf16[8,1792,128]{2,1,0:T(8,128)(2,1)S(1)}, bf16[8,1792,128]{2,1,0:T(8,128)(2,1)}, u32[]{:S(2)}) copy-start(bf16[8,1792,128]{2,1,0:T(8,128)(2,1)} %all-gather.4.cloned.1.call-done.arr) | copy-start | bytes 11010052
  82.7 19.8 %slice-start.1 = ((s8[4718592]{0:T(1024)(128)(4,1)}), s8[524288]{0:T(1024)(128)(4,1)S(1)}, s32[]{:S(2)}) async-start(s8[4718592]{0:T(1024)(128)(4,1)} %bitcast.18), calls=%async_computation.7 | async-start | bytes 1048576
  82.7 19.8 %copy-start = (bf16[1,3072,768]{2,1,0:T(8,128)(2,1)S(1)}, bf16[1,3072,768]{2,1,0:T(8,128)(2,1)}, u32[]{:S(2)}) copy-start(bf16[1,3072,768]{2,1,0:T(8,128)(2,1)} %param.18) | copy-start | bytes 14155780
  94.5 15.5 %copy-start.10 = (bf16[768,2304]{1,0:T(8,128)(2,1)}, bf16[768,2304]{1,0:T(8,128)(2,1)S(1)}, u32[]{:S(2)}) copy-start(bf16[768,2304]{1,0:T(8,128)(2,1)S(1)} %get-tuple-element.32.normed_t) | copy-start | bytes 10616836
  94.6 15.5 %copy-start.11 = (bf16[384,2304]{1,0:T(8,128)(2,1)}, bf16[384,2304]{1,0:T(8,128)(2,1)S(1)}, u32[]{:S(2)}) copy-start(bf16[384,2304]{1,0:T(8,128)(2,1)S(1)} %get-tuple-element.33.hidden_t) | copy-start | bytes 5308420
  94.6 15.5 %copy-start.12 = (bf16[2304,384]{1,0:T(8,128)(2,1)}, bf16[2304,384]{1,0:T(8,128)(2,1)S(1)}, u32[]{:S(2)}) copy-start(bf16[2304,384]{1,0:T(8,128)(2,1)S(1)} %get-tuple-element.30.slope) | copy-start | bytes 5308420
  94.7 15.4 %copy-start.2 = (bf16[512,768]{1,0:T(8,128)(2,1)}, bf16[512,768]{1,0:T(8,128)(2,1)S(1)}, u32[]{:S(2)}) copy-start(bf16[512,768]{1,0:T(8,128)(2,1)S(1)} %shard_map.133.near) | copy-start | bytes 2359300
  94.7 7.8 %collective-permute-start.6 = (bf16[512,768]{1,0:T(8,128)(2,1)S(1)}, bf16[512,768]{1,0:T(8,128)(2,1)S(1)}, u32[]{:S(2)}, u32[]{:S(2)}) collective-permute-start(bf16[512,768]{1,0:T(8,128)(2,1)S(1)} %shard_map.133.near), channel_id=1, source_target_pairs={{0,1},{1,0},{2,3},{3,2},{4,5},{5,4},{6,7},{7,6},{8,9},{9,8},{10,11... | collective-permute-start | bytes 2359304 | tf_op jit(solution)/shard_map/ppermute | solution.py:574
  102.5 7.6 %copy-start.9 = (f32[3]{0:T(128)}, f32[3]{0:T(128)S(1)}, u32[]{:S(2)}) copy-start(f32[3]{0:T(128)S(1)} %pad_maximum_fusion.scalars) | copy-start | bytes 40
  102.5 7.6 %copy-start.4 = (bf16[512,768]{1,0:T(8,128)(2,1)}, bf16[512,768]{1,0:T(8,128)(2,1)S(1)}, u32[]{:S(2)}) copy-start(bf16[512,768]{1,0:T(8,128)(2,1)S(1)} %collective-permute-done.6.far) | copy-start | bytes 2359300
  110.1 4.3 %copy-start.13 = (f32[8,128]{1,0:T(8,128)}, f32[8,128]{1,0:T(8,128)S(1)}, u32[]{:S(2)}) copy-start(f32[8,128]{1,0:T(8,128)S(1)} %get-tuple-element.31._) | copy-start | bytes 12292
  110.1 20.3 %all-to-all-start.3 = ((bf16[32,56,128]{2,1,0:T(8,128)(2,1)}), bf16[32,56,128]{2,1,0:T(8,128)(2,1)S(1)}, u32[]{:S(2)}, u32[]{:S(2)}) async-start(bf16[32,56,128]{2,1,0:T(8,128)(2,1)} %bitcast.11), calls=%async_computation.3 | async-start | bytes 917504 | tf_op jit(solution)/shard_map/all_to_all | solution.py:563
  114.4 16.1 %copy-start.5 = (f32[132,1]{1,0:T(8,128)S(1)}, f32[132,1]{1,0:T(8,128)}, u32[]{:S(2)}) copy-start(f32[132,1]{1,0:T(8,128)} %get-tuple-element.29.slot) | copy-start | bytes 1588
  130.5 0.7 copy-start.8
Sparse Core Ops, SparseCore 0:
  34.5 33.0 all-gather.3
  69.9 38.7 all-gather.5
